TPU v7x, 128 devices: a whole 4x4x4 slice. The times are simulated.
128 devices in a mesh: tm: 32 (over y, z, core), mp: 4 (over x).
Axes of the slice: x: 4, y: 4, z: 4, core: 2. Of those that a mesh axis runs over, the one named last changes fastest.
Arguments:
- tokens: bfloat16 [32768, 2048], P('tm'), may hold values from -6 to 6
- gain_self: bfloat16 [2048], replicated, may hold values from 0.099609375 to 1.8984375
- gain_cross: bfloat16 [2048], replicated, may hold values from 0.099609375 to 1.8984375
- w_query: bfloat16 [2048, 2048], P(None, 'mp'), may hold values from -0.6629126 to 0.6629126
- w_key: bfloat16 [2048, 2048], P(None, 'mp'), may hold values from -0.6629126 to 0.6629126
- w_value: bfloat16 [2048, 2048], P(None, 'mp'), may hold values from -0.125 to 0.125
- w_out: bfloat16 [2048, 2048], P('mp'), may hold values from -0.125 to 0.125
- w_cross_query: bfloat16 [2048, 2048], P(None, 'mp'), may hold values from -0.6629126 to 0.6629126
- w_cross_out: bfloat16 [2048, 2048], P('mp'), may hold values from -0.125 to 0.125
- w_text_key: bfloat16 [1024, 2048], P(None, 'mp'), may hold values from -0.9375 to 0.9375
- w_text_value: bfloat16 [1024, 2048], P(None, 'mp'), may hold values from -0.1875 to 0.1875
- text_states: bfloat16 [64, 512, 1024], P('tm'), may hold values from -6 to 6
- song_of_block: int32 [64], replicated, may hold values from 0 to 31, never falling along the last dimension, each value on 1 to 4 neighbouring positions
- last_fill: int32 [32], replicated, may hold values from 1 to 512
Outputs:
- mixed: bfloat16 [32768, 2048], P('tm', 'mp')
Inputs may be any that keep to these rules, and one draw needn't show every extreme that they name: `song_of_block`: song ids never fall along the blocks; each song covers 1 to 4 consecutive blocks, one exactly 4.
All inputs are finite; a program needn't handle non-finite values.
Results may differ from a plain program's by a relative error of at most 0.025.
Values may be sent and summed in bfloat16 or wider, within the bound.
A program may use at most 192 MiB of HBM per device.

v0:
```python
import jax
import jax.numpy as jnp
from jax import lax
from jax.sharding import PartitionSpec as P

HD = 64


epsilon = 1e-05


def shifted(shard, axis, by):
    count = lax.axis_size(axis)
    pairs = [(i, i + by) for i in range(count) if 0 <= i + by < count]
    return lax.ppermute(shard, axis, pairs)


def entering(part, axis, combine, identity):
    place = lax.axis_index(axis)
    gathered = jax.tree.map(lambda a: lax.all_gather(a, axis), part)
    state = jax.tree.map(lambda a, e: jnp.zeros_like(a) + jnp.asarray(e, a.dtype), part, identity)

    def one(step, state):
        return combine(
            state, jax.tree.map(lambda a: lax.dynamic_index_in_dim(a, step, 0, False), gathered)
        )

    return lax.fori_loop(0, place, one, state)


def normalize(values, gain):
    meansq = jnp.mean(values * values, axis=-1, keepdims=True)
    return values * lax.rsqrt(meansq + epsilon) * gain.astype(jnp.float32)


def attend(query, keys, value_rows, allowed, head_dim):
    heads = query.shape[1] // head_dim
    query_heads = query.reshape(query.shape[0], heads, head_dim)
    key_heads = keys.reshape(keys.shape[0], heads, head_dim)
    value_heads = value_rows.reshape(value_rows.shape[0], heads, head_dim)
    scores = jnp.einsum(
        "qhd,khd->hqk", query_heads, key_heads, preferred_element_type=jnp.float32
    ) * head_dim ** (-0.5)
    if allowed is not None:
        scores = jnp.where(allowed[None], scores, -1e30)
    top = jnp.max(scores, axis=-1, keepdims=True)
    weights = jnp.exp(scores - top)
    probs = (weights / jnp.sum(weights, axis=-1, keepdims=True)).astype(jnp.bfloat16)
    mixed = jnp.einsum("hqk,khd->qhd", probs, value_heads, preferred_element_type=jnp.float32)
    return mixed.reshape(query.shape[0], heads * head_dim).astype(jnp.bfloat16)


def keep_later(earlier, later):
    taken = later[0][0] > 0.5
    return (jnp.maximum(earlier[0], later[0]), jnp.where(taken, later[1], earlier[1]))


def on_device(
    tokens,
    gain_self,
    gain_cross,
    w_query,
    w_key,
    w_value,
    w_out,
    w_cross_query,
    w_cross_out,
    w_text_key,
    w_text_value,
    text_states,
    song_of_block,
    last_fill,
):
    rows, width = tokens.shape
    slots, text_len, text_width = text_states.shape
    block = rows // slots
    cols = w_query.shape[1]
    device = lax.axis_index("tm")
    start_block = device * slots
    song_count = last_fill.shape[0]
    is_last = jnp.concatenate([song_of_block[1:] != song_of_block[:-1], jnp.ones((1,), bool)])
    match = song_of_block[:, None] == jnp.arange(song_count, dtype=jnp.int32)[None, :]
    fill_song = jnp.sum(jnp.where(match, last_fill[None, :], 0), axis=1)
    filled_all = jnp.where(is_last, fill_song, block)
    my_songs = lax.dynamic_slice_in_dim(song_of_block, start_block, slots)
    my_filled = lax.dynamic_slice_in_dim(filled_all, start_block, slots)
    earlier_song = jnp.where(device > 0, song_of_block[jnp.maximum(start_block - 1, 0)], -1)
    before = jnp.concatenate([earlier_song.reshape(1), my_songs[:-1]])
    starts = my_songs != before
    slot_ids = jnp.arange(slots, dtype=jnp.int32)
    latest = lax.cummax(jnp.where(starts, slot_ids, -1), axis=0)
    normed = normalize(tokens.astype(jnp.float32), gain_self).astype(jnp.bfloat16)
    query = jnp.dot(normed, w_query, preferred_element_type=jnp.float32).astype(jnp.bfloat16)
    keys = jnp.dot(normed, w_key, preferred_element_type=jnp.float32).astype(jnp.bfloat16)
    value_rows = jnp.dot(normed, w_value, preferred_element_type=jnp.float32).astype(jnp.bfloat16)
    own_pairs = jnp.concatenate([keys, value_rows], axis=1)
    previous = shifted(own_pairs[rows - block :], "tm", 1)
    pair_all = jnp.concatenate([previous, own_pairs], axis=0)
    position = jnp.arange(block, dtype=jnp.int32)
    pieces = []
    for slot in range(slots):
        window = pair_all[slot * block : (slot + 2) * block]
        same = before[slot] == my_songs[slot]
        allowed_prev = same & (position[None, :] > position[:, None])
        allowed_own = (position[None, :] <= position[:, None]) & (
            position[None, :] < my_filled[slot]
        )
        allowed = jnp.concatenate([allowed_prev, allowed_own], axis=1)
        pieces.append(
            attend(
                query[slot * block : (slot + 1) * block],
                window[:, :cols],
                window[:, cols:],
                allowed,
                HD,
            )
        )
    context = jnp.concatenate(pieces, axis=0)
    partial_self = jnp.dot(context, w_out, preferred_element_type=jnp.float32)
    share = width // lax.axis_size("mp")
    offset = lax.axis_index("mp") * share
    summed = lax.psum(partial_self.astype(jnp.bfloat16), "mp").astype(jnp.float32)
    hidden = tokens.astype(jnp.float32) + summed
    normed_cross = normalize(hidden, gain_cross).astype(jnp.bfloat16)
    hidden_share = lax.dynamic_slice_in_dim(hidden, offset, share, 1)
    cross_query = jnp.dot(normed_cross, w_cross_query, preferred_element_type=jnp.float32).astype(
        jnp.bfloat16
    )
    text_weights = jnp.concatenate([w_text_key, w_text_value], axis=1)
    flat_text = text_states.reshape(slots * text_len, text_width)
    projected = (
        jnp.dot(flat_text, text_weights, preferred_element_type=jnp.float32)
        .astype(jnp.bfloat16)
        .reshape(slots, text_len, 2 * cols)
    )
    newest = latest[slots - 1]
    carried = projected[jnp.maximum(newest, 0)]
    begun = jnp.any(starts).astype(jnp.bfloat16).reshape(1)
    arrived = entering(
        (begun, carried), "tm", keep_later, (jnp.zeros((1,), jnp.bfloat16), jnp.zeros_like(carried))
    )
    incoming = arrived[1]
    cross_pieces = []
    for slot in range(slots):
        source = latest[slot]
        text_pair = jnp.where(source >= 0, projected[jnp.maximum(source, 0)], incoming)
        cross_pieces.append(
            attend(
                cross_query[slot * block : (slot + 1) * block],
                text_pair[:, :cols],
                text_pair[:, cols:],
                None,
                HD,
            )
        )
    cross_context = jnp.concatenate(cross_pieces, axis=0)
    partial_cross = jnp.dot(cross_context, w_cross_out, preferred_element_type=jnp.float32)
    cross_summed = lax.psum_scatter(
        partial_cross.astype(jnp.bfloat16), "mp", scatter_dimension=1, tiled=True
    ).astype(jnp.float32)
    return (hidden_share + cross_summed).astype(jnp.bfloat16)


def solution(mesh):
    in_specs = (
        P("tm", None),
        P(),
        P(),
        P(None, "mp"),
        P(None, "mp"),
        P(None, "mp"),
        P("mp", None),
        P(None, "mp"),
        P("mp", None),
        P(None, "mp"),
        P(None, "mp"),
        P("tm", None, None),
        P(),
        P(),
    )
    out_specs = P("tm", "mp")
    return jax.shard_map(
        on_device, mesh=mesh, in_specs=in_specs, out_specs=out_specs, check_vma=False
    )
```

profile of v0, /device:TPU:1, one launch (start us, length us, event | category | flops | bytes accessed | tf_op | source)
XLA Modules:
  0.0 379.5 jit_solution(11569126951032162312)
XLA Ops:
  8.2 3.4 fusion.6
  11.6 4.3 %convolution_convert_fusion.3 = bf16[1024,512]{0,1:T(8,128)(2,1)S(1)} fusion(bf16[2048,512]{1,0:T(8,128)(2,1)} %param.21, bf16[1024,2048]{1,0:T(8,128)(2,1)S(1)} %copy-done.2, f32[2048]{0:T(1024)S(1)} %convert_element_type.99, f32[1024]{0:T(1024)S(1)} %add_rsqrt_fusion.1), kind=kOutput, calls=%fused_computation.57 | convolution fusion | flops 2156396544 | bytes 7352320 | tf_op jit(solution)/shard_map/dot_general | solution.py:95
  16.0 2.6 convolution_convert_fusion.4
  18.6 1.0 copy-done.6
  19.6 1.1 pad_maximum_fusion.3
  20.7 5.1 %collective-permute-start = (bf16[512,1024]{0,1:T(8,128)(2,1)}, bf16[512,1024]{0,1:T(8,128)(2,1)}, u32[]{:S(2)}, u32[]{:S(2)}) collective-permute-start(bf16[512,1024]{0,1:T(8,128)(2,1)} %pad_maximum_fusion.3), channel_id=1, source_target_pairs={{0,4},{4,8},{8,12},{12,16},{16,20},{20,24},{24,28},{28,32},{32,36}... | collective-permute-start | bytes 3145736 | tf_op jit(solution)/shard_map/ppermute | solution.py:15
  28.2 5.4 %convolution_convert_fusion.2 = bf16[1024,512]{0,1:T(8,128)(2,1)S(1)} fusion(bf16[2048,512]{1,0:T(8,128)(2,1)} %param.19, bf16[1024,2048]{1,0:T(8,128)(2,1)} %param.16, f32[2048]{0:T(1024)S(1)} %convert_element_type.99, f32[1024]{0:T(1024)S(1)} %add_rsqrt_fusion.1), kind=kOutput, calls=%fused_computation.56 | convolution fusion | flops 2156396544 | bytes 7352320 | tf_op jit(solution)/shard_map/dot_general | solution.py:93
  33.6 1.1 fusion.76
  36.9 10.5 %fusion.80 = (f32[8,512]{1,0:T(8,128)S(1)}, f32[8,512,1024]{2,1,0:T(8,128)}) fusion(pred[512,1024]{1,0:T(8,128)(4,1)} %pad_add_fusion.1, bf16[512,8,64]{0,2,1:T(8,128)(2,1)} %bitcast.94, bf16[1024,8,64]{0,2,1:T(8,128)(2,1)} %bitcast.84), kind=kOutput, calls=%fused_computation.113 | convolution fusion | flops 553649152 | bytes 18890752 | tf_op jit(solution)/shard_map/sub | solution.py:47
  47.4 9.3 %fusion.40 = bf16[8,64,512]{2,1,0:T(8,128)(2,1)} fusion(bf16[1024,8,64]{0,2,1:T(8,128)(2,1)S(1)} %bitcast.83, f32[8,512,1024]{2,1,0:T(8,128)} %get-tuple-element.83, f32[8,512]{1,0:T(8,128)S(1)} %get-tuple-element.82), kind=kOutput, calls=%fused_computation.61 | convolution fusion | flops 545521664 | bytes 18366464 | tf_op jit(solution)/shard_map/hqk,khd->qhd/dot_general | solution.py:49
  60.2 3.1 pad_maximum_fusion
  63.2 10.8 %fusion.81 = (f32[8,512]{1,0:T(8,128)S(1)}, f32[8,512,1024]{2,1,0:T(8,128)}) fusion(pred[512,1024]{1,0:T(8,128)(4,1)} %pad_add_fusion, bf16[512,8,64]{0,2,1:T(8,128)(2,1)} %bitcast.93, bf16[1024,8,64]{0,2,1:T(8,128)(2,1)} %bitcast.86), kind=kOutput, calls=%fused_computation.114 | convolution fusion | flops 553649152 | bytes 18890752 | tf_op jit(solution)/shard_map/sub | solution.py:47
  74.1 8.5 %fusion.41 = bf16[8,64,512]{2,1,0:T(8,128)(2,1)S(1)} fusion(bf16[1024,8,64]{0,2,1:T(8,128)(2,1)S(1)} %bitcast.85, f32[8,512,1024]{2,1,0:T(8,128)} %get-tuple-element.85, f32[8,512]{1,0:T(8,128)S(1)} %get-tuple-element.84), kind=kOutput, calls=%fused_computation.62 | convolution fusion | flops 545521664 | bytes 18366464 | tf_op jit(solution)/shard_map/hqk,khd->qhd/dot_general | solution.py:49
  82.6 4.4 %convolution_convert_fusion.1 = bf16[1024,2048]{1,0:T(8,128)(2,1)} fusion(bf16[512,2048]{1,0:T(8,128)(2,1)S(1)} %copy-done, bf16[512,512]{0,1:T(8,128)(2,1)S(1)} %bitcast.96, bf16[512,512]{0,1:T(8,128)(2,1)S(1)} %bitcast.98), kind=kOutput, calls=%fused_computation.46 | convolution fusion | flops 2151677952 | bytes 7340032 | tf_op jit(solution)/shard_map/dot_general | solution.py:119
  89.4 4.2 %fusion.34 = bf16[1024,1024]{0,1:T(8,128)(2,1)S(1)} fusion(bf16[1024,1024]{1,0:T(8,128)(2,1)} %bitcast.95, bf16[1024,512]{1,0:T(8,128)(2,1)S(1)} %copy-done.14, bf16[1024,512]{1,0:T(8,128)(2,1)} %param.25), kind=kOutput, calls=%fused_computation.54 | convolution fusion | flops 2152726528 | bytes 6291456 | tf_op jit(solution)/shard_map/dot_general | solution.py:132
  93.6 1.1 constant_dynamic-slice_fusion.1
  97.3 63.2 %all-reduce = bf16[32]{0:T(256)(128)(2,1)S(1)} all-reduce(bf16[32]{0:T(256)(128)(2,1)S(1)} %dynamic-update-slice), channel_id=1, replica_groups=mesh['tm'=32,'mp'=4] {'tm'}, use_global_device_ids=true, to_apply=%add | all-reduce | flops 32 | bytes 128
  162.3 19.2 %all-reduce.3.cloned.1.call-done = bf16[1024,2048]{1,0:T(8,128)(2,1)} async-done(((bf16[1024,2048]{1,0:T(8,128)(2,1)}), bf16[1024,2048]{1,0:T(8,128)(2,1)}) %all-reduce.3.cloned.1.call-update) | async-done | bytes 4194320 | tf_op jit(solution)/shard_map/psum | solution.py:122
  181.4 9.1 %convert_add_fusion = (f32[1024,2048]{1,0:T(8,128)}, f32[1024]{0:T(1024)S(1)}) fusion(bf16[1024,2048]{1,0:T(8,128)(2,1)} %param.16, bf16[1024,2048]{1,0:T(8,128)(2,1)} %all-reduce.3.cloned.1.call-done), kind=kLoop, calls=%fused_computation.14 | loop fusion | flops 10484736 | bytes 16781312 | tf_op jit(solution)/shard_map/add | solution.py:123
  191.2 2.7 fusion.37
  193.9 1.1 fusion.74
  195.0 16.0 %all-gather.2.cloned.1.call-done = bf16[32,512,1024]{2,1,0:T(8,128)(2,1)} async-done(((bf16[1,512,1024]{2,1,0:T(8,128)(2,1)}), bf16[32,512,1024]{2,1,0:T(8,128)(2,1)}) %all-gather.2.cloned.1.call-update) | async-done | bytes 33554448 | tf_op jit(solution)/shard_map/all_gather | solution.py:20
  211.1 3.0 while.12
  211.7 2.1 bitcast_select_fusion.4
  214.1 1.7 bitcast_select_fusion.2
  216.9 7.1 %fusion.82 = (f32[8,512]{1,0:T(8,128)S(1)}, f32[8,512,512]{1,2,0:T(8,128)}) fusion(bf16[512,8,64]{0,2,1:T(8,128)(2,1)} %bitcast.92, bf16[512,8,64]{0,2,1:T(8,128)(2,1)S(1)} %bitcast.90), kind=kOutput, calls=%fused_computation.115 | convolution fusion | flops 274727424 | bytes 9453568 | tf_op jit(solution)/shard_map/sub | solution.py:47
  224.0 5.0 %fusion.83 = (f32[8,512]{1,0:T(8,128)S(1)}, f32[8,512,512]{1,2,0:T(8,128)}) fusion(bf16[512,8,64]{0,2,1:T(8,128)(2,1)S(1)} %bitcast.91, bf16[512,8,64]{0,2,1:T(8,128)(2,1)S(1)} %bitcast.89), kind=kOutput, calls=%fused_computation.116 | convolution fusion | flops 274727424 | bytes 9453568 | tf_op jit(solution)/shard_map/sub | solution.py:47
  229.0 4.4 %fusion.38 = bf16[8,64,512]{2,1,0:T(8,128)(2,1)S(1)} fusion(bf16[512,8,64]{0,2,1:T(8,128)(2,1)S(1)} %bitcast.88, f32[8,512,512]{1,2,0:T(8,128)} %get-tuple-element.87, f32[8,512]{1,0:T(8,128)S(1)} %get-tuple-element.86), kind=kOutput, calls=%fused_computation.59 | convolution fusion | flops 272891904 | bytes 9453568 | tf_op jit(solution)/shard_map/hqk,khd->qhd/dot_general | solution.py:49
  233.4 1.4 copy-done.18
  236.4 4.3 %convolution_convert_fusion = bf16[1024,2048]{1,0:T(8,128)(2,1)} fusion(bf16[512,2048]{1,0:T(8,128)(2,1)S(1)} %copy-done.13, bf16[512,512]{0,1:T(8,128)(2,1)S(1)} %bitcast.97, bf16[512,512]{0,1:T(8,128)(2,1)S(1)} %bitcast.99), kind=kOutput, calls=%fused_computation.45 | convolution fusion | flops 2151677952 | bytes 7340032 | tf_op jit(solution)/shard_map/dot_general | solution.py:157
  240.7 127.7 %reduce-scatter.2.cloned.1.call-done = bf16[1024,512]{1,0:T(8,128)(2,1)} async-done(((bf16[1024,2048]{1,0:T(8,128)(2,1)}), bf16[1024,512]{1,0:T(8,128)(2,1)}) %reduce-scatter.2.cloned.1.call-update) | async-done | bytes 1048592 | tf_op jit(solution)/shard_map/reduce_scatter | solution.py:158
  368.4 3.2 add_convert_fusion
  (76 shorter events, 14.0 us)
Async XLA Ops:
  7.4 75.3 %copy-start = (bf16[512,2048]{1,0:T(8,128)(2,1)S(1)}, bf16[512,2048]{1,0:T(8,128)(2,1)}, u32[]{:S(2)}) copy-start(bf16[512,2048]{1,0:T(8,128)(2,1)} %param.22) | copy-start | bytes 6291460
  7.4 174.0 %all-reduce.3.cloned.1.call-start = ((), (), s32[]{:S(2)}) async-start(), calls=%async_computation.1 | async-start | bytes 8388608 | tf_op jit(solution)/shard_map/psum | solution.py:122
  7.4 4.3 %copy-start.2 = (bf16[1024,2048]{1,0:T(8,128)(2,1)S(1)}, bf16[1024,2048]{1,0:T(8,128)(2,1)}, u32[]{:S(2)}) copy-start(bf16[1024,2048]{1,0:T(8,128)(2,1)} %param.16) | copy-start | bytes 12582916
  11.6 4.3 %copy-start.11 = (bf16[2048,512]{1,0:T(8,128)(2,1)S(1)}, bf16[2048,512]{1,0:T(8,128)(2,1)}, u32[]{:S(2)}) copy-start(bf16[2048,512]{1,0:T(8,128)(2,1)} %param.20) | copy-start | bytes 6291460
  16.0 9.8 %copy-start.10 = (s32[64]{0:T(128)S(1)}, s32[64]{0:T(128)}, u32[]{:S(2)}) copy-start(s32[64]{0:T(128)} %param.28) | copy-start | bytes 772
  16.0 10.6 %copy-start.15 = (s32[32]{0:T(128)S(1)}, s32[32]{0:T(128)}, u32[]{:S(2)}) copy-start(s32[32]{0:T(128)} %param.29) | copy-start | bytes 388
  18.6 1.0 copy-start.6
  20.7 39.5 %collective-permute-start = (bf16[512,1024]{0,1:T(8,128)(2,1)}, bf16[512,1024]{0,1:T(8,128)(2,1)}, u32[]{:S(2)}, u32[]{:S(2)}) collective-permute-start(bf16[512,1024]{0,1:T(8,128)(2,1)} %pad_maximum_fusion.3), channel_id=1, source_target_pairs={{0,4},{4,8},{8,12},{12,16},{16,20},{20,24},{24,28},{28,32},{32,36}... | collective-permute-start | bytes 3145736 | tf_op jit(solution)/shard_map/ppermute | solution.py:15
  63.2 10.8 %copy-start.7 = (bf16[1024,512]{0,1:T(8,128)(2,1)S(1)}, bf16[1024,512]{0,1:T(8,128)(2,1)}, u32[]{:S(2)}) copy-start(bf16[1024,512]{0,1:T(8,128)(2,1)} %get-tuple-element.65) | copy-start | bytes 3145732
  74.1 8.6 %copy-start.16 = (bf16[8,64,512]{2,1,0:T(8,128)(2,1)S(1)}, bf16[8,64,512]{2,1,0:T(8,128)(2,1)}, u32[]{:S(2)}) copy-start(bf16[8,64,512]{2,1,0:T(8,128)(2,1)} %fusion.40) | copy-start | bytes 1572868
  87.1 2.3 copy-start.14
  87.1 123.9 %all-gather.2.cloned.1.call-start = ((), (), s32[]{:S(2)}) async-start(), calls=%async_computation.2 | async-start | bytes 34603008 | tf_op jit(solution)/shard_map/all_gather | solution.py:20
  89.4 6.7 %copy-start.17 = (u32[128]{0:T(128)S(1)}, u32[128]{0:T(128)}, u32[]{:S(2)}) copy-start(u32[128]{0:T(128)} %constant.78) | copy-start | bytes 1540
  89.4 72.9 %copy-start.9 = (bf16[2048]{0:T(1024)(128)(2,1)S(1)}, bf16[2048]{0:T(1024)(128)(2,1)}, u32[]{:S(2)}) copy-start(bf16[2048]{0:T(1024)(128)(2,1)} %param.18) | copy-start | bytes 12292
  93.6 97.0 %copy-start.4 = (bf16[1024,1024]{0,1:T(8,128)(2,1)}, bf16[1024,1024]{0,1:T(8,128)(2,1)S(1)}, u32[]{:S(2)}) copy-start(bf16[1024,1024]{0,1:T(8,128)(2,1)S(1)} %fusion.34) | copy-start | bytes 6291460
  94.7 273.7 %reduce-scatter.2.cloned.1.call-start = ((), (), s32[]{:S(2)}) async-start(), calls=%async_computation.3 | async-start | bytes 5242880 | tf_op jit(solution)/shard_map/reduce_scatter | solution.py:158
  181.4 9.2 %copy-start.3 = (bf16[1024,2048]{1,0:T(8,128)(2,1)S(1)}, bf16[1024,2048]{1,0:T(8,128)(2,1)}, u32[]{:S(2)}) copy-start(bf16[1024,2048]{1,0:T(8,128)(2,1)} %param.16) | copy-start | bytes 12582916
  181.4 9.2 %copy-start.5 = (bf16[1024,2048]{1,0:T(8,128)(2,1)S(1)}, bf16[1024,2048]{1,0:T(8,128)(2,1)}, u32[]{:S(2)}) copy-start(bf16[1024,2048]{1,0:T(8,128)(2,1)} %all-reduce.3.cloned.1.call-done) | copy-start | bytes 12582916
  181.4 9.8 %copy-start.12 = (bf16[2048,512]{1,0:T(8,128)(2,1)S(1)}, bf16[2048,512]{1,0:T(8,128)(2,1)}, u32[]{:S(2)}) copy-start(bf16[2048,512]{1,0:T(8,128)(2,1)} %param.23) | copy-start | bytes 6291460
  216.9 7.2 %copy-start.8 = (bf16[512,512]{0,1:T(8,128)(2,1)S(1)}, bf16[512,512]{0,1:T(8,128)(2,1)}, u32[]{:S(2)}) copy-start(bf16[512,512]{0,1:T(8,128)(2,1)} %get-tuple-element.68) | copy-start | bytes 1572868
  229.0 5.8 %copy-start.18 = (f32[8,512,512]{1,2,0:T(8,128)S(1)}, f32[8,512,512]{1,2,0:T(8,128)}, u32[]{:S(2)}) copy-start(f32[8,512,512]{1,2,0:T(8,128)} %get-tuple-element.89) | copy-start | bytes 25165828
  234.8 1.6 copy-start.13
  240.7 130.9 %copy-start.1 = (bf16[512,2048]{1,0:T(8,128)(2,1)S(1)}, bf16[512,2048]{1,0:T(8,128)(2,1)}, u32[]{:S(2)}) copy-start(bf16[512,2048]{1,0:T(8,128)(2,1)} %param.22) | copy-start | bytes 6291460
Sparse Core Ops, SparseCore 0:
  87.2 94.1 all-reduce.2
  240.9 127.5 reduce-scatter.1
Sparse Core Ops, SparseCore 1:
  94.8 116.1 all-gather.1
where the time goes:
time: 386 us; the launch traced here: 380 us
  waiting for transfers between devices  163 us (42%)
  matrix products  84.5 us (22%)
  blocking collectives  63.2 us (16%)
  other arithmetic  30.4 us (8%)
  between operations  21.1 us (5%)
  local copies, waits for them, and re-layouts  12.1 us (3%)
  starting transfers between devices  5.18 us (1%)
    reduce_scatter x1, waiting for transfers between devices, on_device(): lax.psum_scatter(partial_cross.astype(jnp.bfloat16), 'mp', scatter_dimens...  128 us
    unnamed x1, blocking collectives  63.2 us
    sub x4, matrix products, attend(): weights = jnp.exp(scores - top)  33.5 us
    dot_general x4, matrix products, attend(): jnp.einsum('hqk,khd->qhd', probs, value_heads, preferred_element_type=jnp...  23.1 us
    psum x1, waiting for transfers between devices, on_device(): lax.psum(partial_self.astype(jnp.bfloat16), 'mp').astype(jnp.float32)  19.2 us
    all_gather x1, waiting for transfers between devices, entering(): gathered = jax.tree.map(lambda a: lax.all_gather(a, axis), part)  16 us
    add x1, other arithmetic, on_device(): hidden = tokens.astype(jnp.float32) + summed  9.15 us
  transfers between devices with their start and end apart: 4, of which 3 were waited for; matrix products, arithmetic and copies ran while one was open for 14% of the time, Pallas kernels for 0%

commit v1 on v0

v1 whole, which is shorter than its diff:
```python
import jax
import jax.numpy as jnp
from jax import lax
from jax.experimental import pallas as pl
from jax.experimental.pallas import tpu as pltpu
from jax.sharding import PartitionSpec as P

F32 = jnp.float32
BF16 = jnp.bfloat16
EPS = 1e-05
MESH = pl.DeviceIdType.MESH
BLK = 512
TILE = 256
COLS = 512
WIDTH = 2048
CHUNKS = ((1, 0), (1, 1), (0, 0), (0, 1))
REMOTE = 80


def dot(a, b):
    return jnp.dot(a, b, preferred_element_type=F32)


def dot_t(a, b):
    return lax.dot_general(a, b, (((1,), (1,)), ((), ())), preferred_element_type=F32)


def kernel(
    tokens, gain_s, gain_c, w_q, w_k, w_v, w_o, w_cq, w_co, w_tk, w_tv, text, song, fill,
    out,
    tok, nrm, wq, wk, wv, wo, wcq, wco, wtk, wtv, txt, tin, ta, tb,
    q, k, v, kp, vp, ctx, hid, acc, part, rs1, rs2, fwd, tk, tv, bias, cc, ob,
    lsem, ssem, rsem,
):
    t, x = lax.axis_index("tm"), lax.axis_index("mp")
    core, y = lax.rem(t, 2), t // 8
    right, left, across = lax.rem(x + 1, 4), lax.rem(x + 3, 4), lax.rem(x + 2, 4)
    to_right, to_left = {"mp": right}, {"mp": left}
    up, down = {"tm": lax.rem(t + 8, 32)}, {"tm": lax.rem(t + 24, 32)}
    next1, next2 = {"tm": lax.rem(t + 1, 32)}, {"tm": lax.rem(t + 2, 32)}
    prev1, prev2 = {"tm": lax.rem(t + 31, 32)}, {"tm": lax.rem(t + 30, 32)}
    sibling = {"tm": t + 1 - 2 * core}

    loads = {}

    def load(name, src, dst):
        copy = pltpu.make_async_copy(src, dst, lsem.at[len(loads)])
        copy.start()
        loads[name] = copy

    def loaded(*names):
        for name in names:
            loads[name].wait()

    barrier = pltpu.get_barrier_semaphore()
    for peer in (prev1, prev2, to_right, to_left, up, down, sibling):
        pl.semaphore_signal(barrier, inc=1, device_id=peer, device_id_type=MESH)
    load("tok1", tokens.at[pl.ds(BLK, BLK)], tok.at[pl.ds(BLK, BLK)])
    load("wk", w_k, wk)
    load("wv", w_v, wv)
    load("tok0", tokens.at[pl.ds(0, BLK)], tok.at[pl.ds(0, BLK)])
    load("wq", w_q, wq)
    load("text", text, txt)
    load("wo", w_o, wo.at[x])
    load("wtk", w_tk, wtk)
    load("wtv", w_tv, wtv)
    load("wcq", w_cq, wcq)
    load("wco", w_co, wco)

    sent = []
    count = [0]

    def fresh():
        count[0] += 1
        return count[0] - 1

    def remote(src, dst, to, n):
        return pltpu.make_async_remote_copy(
            src_ref=src, dst_ref=dst, send_sem=ssem.at[n], recv_sem=rsem.at[n],
            device_id=to, device_id_type=MESH,
        )

    def send(src, dst, to, n):
        copy = remote(src, dst, to, n)
        copy.start()
        sent.append(copy)

    def landed(ref, n):
        remote(ref, ref, to_right, n).wait_recv()

    class Gather:
        def __init__(self, me, after, before, src, at):
            self.me, self.after, self.before, self.src, self.at = me, after, before, src, at
            self.n = [fresh() for _ in range(4)]

        def start(self):
            send(self.src, self.at(self.me, None), self.after, self.n[0])
            send(self.src, self.at(self.me, None), self.before, self.n[1])

        def forward(self):
            lo, hi = lax.rem(self.me + 3, 4), lax.rem(self.me + 1, 4)
            landed(self.at(lo, None), self.n[0])
            send(self.at(lo, 0), self.at(lo, 0), self.after, self.n[2])
            landed(self.at(hi, None), self.n[1])
            send(self.at(hi, 1), self.at(hi, 1), self.before, self.n[3])

        def finish(self):
            far = lax.rem(self.me + 2, 4)
            landed(self.at(far, 0), self.n[2])
            landed(self.at(far, 1), self.n[3])

    def halves(ref, half, size):
        return ref if half is None else ref.at[pl.ds(half * size, size)]

    others = [lax.rem(x + d, 4) for d in (1, 3, 2)]
    wo_x = Gather(
        x, to_right, to_left, w_o.at[core, y], lambda i, h: halves(wo.at[i, core, y], h, 32)
    )
    wo_y = [
        Gather(
            y, up, down, wo.at[g, core, y], lambda i, h, g=g: halves(wo.at[g, core, i], h, 32)
        )
        for g in others
    ]
    wo_n = [fresh() for _ in others]
    text_n = [fresh() for _ in range(3)]
    text_x = Gather(x, to_right, to_left, tin.at[x], lambda i, h: halves(tin.at[i], h, 64))
    kv_n = [fresh() for _ in range(2)]

    pl.semaphore_wait(barrier, 7)
    send(text.at[0, x], ta.at[0], next1, text_n[0])
    send(text.at[1, x], ta.at[1], next1, text_n[1])
    send(text.at[1, x], tb, next2, text_n[2])
    wo_x.start()

    b0 = 2 * t
    s0, s1 = song[b0], song[b0 + 1]
    m1 = song[jnp.maximum(b0 - 1, 0)]
    m2 = song[jnp.maximum(b0 - 2, 0)]
    m3 = song[jnp.maximum(b0 - 3, 0)]
    p2 = song[jnp.minimum(b0 + 2, 63)]
    same = [(t > 0) & (m1 == s0), s0 == s1]
    filled = [
        jnp.where(s0 != s1, fill[s0], BLK),
        jnp.where((t == 31) | (p2 != s1), fill[s1], BLK),
    ]
    second_starts = m1 != m2
    first_starts = (t == 1) | (m2 != m3)

    def normed(block):
        gain = gain_s[...].astype(F32)

        @pl.loop(0, BLK // 32)
        def _(i):
            values = tok[pl.ds(pl.multiple_of(block * BLK + i * 32, 32), 32), :].astype(F32)
            meansq = jnp.mean(values * values, axis=-1, keepdims=True)
            nrm[pl.ds(pl.multiple_of(i * 32, 32), 32), :] = (
                values * lax.rsqrt(meansq + EPS) * gain
            ).astype(BF16)

    def project(a, w, dst, row, scale=None):
        @pl.loop(0, COLS // 256)
        def _(i):
            cols = pl.ds(pl.multiple_of(i * 256, 256), 256)
            res = dot(a[...], w[:, cols]).astype(BF16)
            if scale is not None:
                res = res * jnp.asarray(scale, BF16)
            dst[pl.ds(row, a.shape[0]), cols] = res

    loaded("tok1")
    normed(1)
    loaded("wk")
    project(nrm, wk, k, BLK)
    send(k.at[pl.ds(BLK, BLK)], kp, next1, kv_n[0])
    loaded("wv")
    project(nrm, wv, v, BLK)
    send(v.at[pl.ds(BLK, BLK)], vp, next1, kv_n[1])
    wo_x.forward()
    loaded("wq")
    project(nrm, wq, q, BLK, 0.125)
    landed(ta.at[0], text_n[0])
    landed(ta.at[1], text_n[1])
    landed(tb, text_n[2])
    tin[x] = jnp.where(second_starts, ta[1], jnp.where(first_starts, ta[0], tb[...]))
    text_x.start()
    wo_x.finish()
    for gather in wo_y:
        gather.start()
    loaded("tok0")
    normed(0)
    project(nrm, wk, k, 0)
    project(nrm, wv, v, 0)
    project(nrm, wq, q, 0, 0.125)
    text_x.forward()

    lane = lax.broadcasted_iota(jnp.int32, (1, 128), 1)
    pick = [(lane < 64).astype(F32).astype(BF16), (lane >= 64).astype(F32).astype(BF16)]
    ones = jnp.ones((TILE, 128), BF16)

    def softmax_parts(tiles):
        top = tiles[0].max(axis=-1, keepdims=True)
        for s in tiles[1:]:
            top = jnp.maximum(top, s.max(axis=-1, keepdims=True))
        return [jnp.exp(s - top) for s in tiles]

    def with_ones(rows):
        return jnp.concatenate([rows, ones], axis=1)

    def ratio(mixed):
        return mixed[:, :128] / mixed[:, 128:]

    def self_chunk(block, half):
        row = block * BLK + half * TILE
        before_k, before_v = (k, v) if block == 1 else (kp, vp)
        i = lax.broadcasted_iota(jnp.int32, (TILE, BLK), 0) + half * TILE
        j = lax.broadcasted_iota(jnp.int32, (TILE, BLK), 1)
        limit = jnp.where(j <= i, filled[block], jnp.where(same[block], BLK, 0))
        bias[...] = jnp.where(j < limit, 0.0, -1e30)
        lower = lax.broadcasted_iota(jnp.int32, (TILE, TILE), 1) <= lax.broadcasted_iota(
            jnp.int32, (TILE, TILE), 0
        )

        @pl.loop(0, COLS // 128)
        def _(pair):
            cols = pl.ds(pl.multiple_of(pair * 128, 128), 128)
            queries = q[pl.ds(row, TILE), cols]
            halves_out = []
            for head in range(2):
                query = queries * pick[head]
                scores = []
                for tile in range(2):
                    own = pl.ds(block * BLK + tile * TILE, TILE)
                    earlier = pl.ds(tile * TILE, TILE)
                    if tile < half:
                        s = dot_t(query, k[own, cols])
                    elif tile > half:
                        s = dot_t(query, before_k[earlier, cols])
                    else:
                        s = jnp.where(
                            lower,
                            dot_t(query, k[own, cols]),
                            dot_t(query, before_k[earlier, cols]),
                        )
                    scores.append(s + bias[:, tile * TILE : (tile + 1) * TILE])
                weights = softmax_parts(scores)
                mixed = None
                for tile in range(2):
                    own = pl.ds(block * BLK + tile * TILE, TILE)
                    earlier = pl.ds(tile * TILE, TILE)
                    w = weights[tile]
                    if tile < half:
                        terms = [(w, v[own, cols])]
                    elif tile > half:
                        terms = [(w, before_v[earlier, cols])]
                    else:
                        terms = [
                            (jnp.where(lower, w, 0.0), v[own, cols]),
                            (jnp.where(lower, 0.0, w), before_v[earlier, cols]),
                        ]
                    for a, b in terms:
                        term = dot(a.astype(BF16), with_ones(b))
                        mixed = term if mixed is None else mixed + term
                halves_out.append(ratio(mixed))
            ctx[x, pl.ds(row, TILE), cols] = jnp.where(lane < 64, *halves_out).astype(BF16)

    ctx_x = [
        Gather(
            x, to_right, to_left, ctx.at[x, pl.ds(b * BLK + h * TILE, TILE)],
            lambda i, part, r=b * BLK + h * TILE: (
                ctx.at[i, pl.ds(r, TILE)]
                if part is None
                else ctx.at[i, pl.ds(r + part * TILE // 2, TILE // 2)]
            ),
        )
        for b, h in CHUNKS
    ]

    self_chunk(*CHUNKS[0])
    ctx_x[0].start()
    for gather in wo_y:
        gather.forward()
    self_chunk(*CHUNKS[1])
    ctx_x[1].start()
    ctx_x[0].forward()
    for gather, g, n in zip(wo_y, others, wo_n):
        gather.finish()
        send(wo.at[g, core], wo.at[g, core], sibling, n)
    landed(kp, kv_n[0])
    landed(vp, kv_n[1])
    self_chunk(*CHUNKS[2])
    ctx_x[2].start()
    ctx_x[1].forward()
    self_chunk(*CHUNKS[3])
    ctx_x[3].start()
    ctx_x[2].forward()

    text_x.finish()
    loaded("text", "wtk", "wtv")

    @pl.loop(0, 4)
    def _(i):
        first = jnp.where(same[0], tin[i], txt[0, i])
        txt[0, i] = first
        txt[1, i] = jnp.where(same[1], first, txt[1, i])

    for block in (1, 0):
        source = txt[block].reshape(BLK, 1024)

        for w, dst in ((wtk, tk), (wtv, tv)):
            @pl.loop(0, COLS // 256)
            def _(i, w=w, dst=dst, source=source, block=block):
                cols = pl.ds(pl.multiple_of(i * 256, 256), 256)
                rows = txt[block].reshape(BLK, 1024)
                dst[block, :, cols] = dot(rows, w[:, cols]).astype(BF16)
    ctx_x[3].forward()

    rs_n = [[fresh() for _ in range(6)] for _ in CHUNKS]
    low, high = pl.ds(0, TILE // 2), pl.ds(TILE // 2, TILE // 2)

    def cross_chunk(c, block, half):
        row = block * BLK + half * TILE
        rows = pl.ds(row, TILE)

        def hidden_tile(i, total):
            cols = pl.ds(pl.multiple_of(i * 512, 512), 512)
            h = tok[rows, cols].astype(F32)
            for g in range(4):
                h = h + dot(ctx[g, rows, :], wo[g, :, :, :, cols].reshape(COLS, 512))
            hid[:, cols] = h
            return total + jnp.sum(h * h, axis=-1, keepdims=True)

        total = lax.fori_loop(0, WIDTH // 512, hidden_tile, jnp.zeros((TILE, 1), F32))
        scale = lax.rsqrt(total * (1.0 / WIDTH) + EPS)

        @pl.loop(0, WIDTH // 256)
        def _(i):
            cols = pl.ds(pl.multiple_of(i * 256, 256), 256)
            nrm[pl.ds(0, TILE), cols] = (
                hid[:, cols] * scale * gain_c[:, cols].astype(F32)
            ).astype(BF16)

        acc[rows, :] = hid[:, pl.ds(pl.multiple_of(x * 512, 512), 512)]
        project(nrm.at[pl.ds(0, TILE)], wcq, cc, 0, 0.125)

        @pl.loop(0, COLS // 128)
        def _(pair):
            cols = pl.ds(pl.multiple_of(pair * 128, 128), 128)
            queries = cc[:, cols]
            halves_out = []
            for head in range(2):
                query = queries * pick[head]
                scores = [
                    dot_t(query, tk[block, pl.ds(tile * TILE, TILE), cols]) for tile in range(2)
                ]
                weights = softmax_parts(scores)
                mixed = None
                for tile in range(2):
                    term = dot(
                        weights[tile].astype(BF16),
                        with_ones(tv[block, pl.ds(tile * TILE, TILE), cols]),
                    )
                    mixed = term if mixed is None else mixed + term
                halves_out.append(ratio(mixed))
            cc[:, cols] = jnp.where(lane < 64, *halves_out).astype(BF16)

        def term(owner):
            cols = pl.ds(pl.multiple_of(owner * 512, 512), 512)
            return dot(cc[...], wco[:, cols]).astype(BF16)

        n = rs_n[c]
        part[c, 0] = term(across)
        send(part.at[c, 0, low], rs1.at[c, 0], to_right, n[0])
        send(part.at[c, 0, high], rs1.at[c, 1], to_left, n[1])
        part[c, 1] = term(right)
        send(part.at[c, 1, high], rs2.at[c, 0, high], to_right, n[2])
        part[c, 2] = term(left)
        send(part.at[c, 2, low], rs2.at[c, 1, low], to_left, n[3])
        acc[rows, :] = acc[rows, :] + term(x).astype(F32)

    def cross_middle(c):
        n = rs_n[c]
        landed(rs1.at[c, 0], n[0])
        fwd[c, 0] = (part[c, 1, low, :].astype(F32) + rs1[c, 0].astype(F32)).astype(BF16)
        send(fwd.at[c, 0], rs2.at[c, 0, low], to_right, n[4])
        landed(rs1.at[c, 1], n[1])
        fwd[c, 1] = (part[c, 2, high, :].astype(F32) + rs1[c, 1].astype(F32)).astype(BF16)
        send(fwd.at[c, 1], rs2.at[c, 1, high], to_left, n[5])

    stores = []

    def cross_end(c, block, half):
        n = rs_n[c]
        rows = pl.ds(block * BLK + half * TILE, TILE)
        landed(rs2.at[c, 0, high], n[2])
        landed(rs2.at[c, 1, low], n[3])
        landed(rs2.at[c, 0, low], n[4])
        landed(rs2.at[c, 1, high], n[5])
        ob[rows, :] = (acc[rows, :] + rs2[c, 0].astype(F32) + rs2[c, 1].astype(F32)).astype(BF16)
        copy = pltpu.make_async_copy(ob.at[rows], out.at[rows], lsem.at[len(loads) + c])
        copy.start()
        stores.append(copy)

    loaded("wo", "wcq", "wco")
    for g, n in zip(others, wo_n):
        landed(wo.at[g, 1 - core], n)
    for c, chunk in enumerate(CHUNKS):
        ctx_x[c].finish()
        cross_chunk(c, *chunk)
        if c >= 1:
            cross_middle(c - 1)
        if c >= 2:
            cross_end(c - 2, *CHUNKS[c - 2])
    last = len(CHUNKS) - 1
    cross_middle(last)
    cross_end(last - 1, *CHUNKS[last - 1])
    cross_end(last, *CHUNKS[last])
    for copy in sent:
        copy.wait_send()
    for copy in stores:
        copy.wait()


def on_device(
    tokens, gain_self, gain_cross, w_query, w_key, w_value, w_out, w_cross_query, w_cross_out,
    w_text_key, w_text_value, text_states, song_of_block, last_fill,
):
    any_space = pl.BlockSpec(memory_space=pl.ANY)
    vmem = pl.BlockSpec(memory_space=pltpu.VMEM)
    smem = pl.BlockSpec(memory_space=pltpu.SMEM)
    n = len(CHUNKS)

    def buf(*shape, dtype=BF16):
        return pltpu.VMEM(shape, dtype)

    scratch = [
        buf(1024, WIDTH),
        buf(BLK, WIDTH),
        buf(WIDTH, COLS),
        buf(WIDTH, COLS),
        buf(WIDTH, COLS),
        buf(4, 2, 4, 64, WIDTH),
        buf(WIDTH, COLS),
        buf(COLS, WIDTH),
        buf(1024, COLS),
        buf(1024, COLS),
        buf(2, 4, 128, 1024),
        buf(4, 128, 1024),
        buf(2, 128, 1024),
        buf(128, 1024),
        buf(1024, COLS),
        buf(1024, COLS),
        buf(1024, COLS),
        buf(BLK, COLS),
        buf(BLK, COLS),
        buf(4, 1024, COLS),
        buf(TILE, WIDTH, dtype=F32),
        buf(1024, COLS, dtype=F32),
        buf(n, 3, TILE, COLS),
        buf(n, 2, TILE // 2, COLS),
        buf(n, 2, TILE, COLS),
        buf(n, 2, TILE // 2, COLS),
        buf(2, BLK, COLS),
        buf(2, BLK, COLS),
        buf(TILE, BLK, dtype=F32),
        buf(TILE, COLS),
        buf(1024, COLS),
        pltpu.SemaphoreType.DMA((16,)),
        pltpu.SemaphoreType.DMA((REMOTE,)),
        pltpu.SemaphoreType.DMA((REMOTE,)),
    ]
    return pl.pallas_call(
        kernel,
        out_shape=jax.ShapeDtypeStruct((1024, COLS), BF16),
        in_specs=[any_space, vmem, vmem] + [any_space] * 9 + [smem, smem],
        out_specs=any_space,
        scratch_shapes=scratch,
        compiler_params=pltpu.CompilerParams(
            collective_id=0, has_side_effects=True, vmem_limit_bytes=62 * 2**20
        ),
    )(
        tokens, gain_self.reshape(1, WIDTH), gain_cross.reshape(1, WIDTH), w_query, w_key, w_value,
        w_out.reshape(2, 4, 64, WIDTH), w_cross_query, w_cross_out, w_text_key, w_text_value,
        text_states.reshape(2, 4, 128, 1024), song_of_block, last_fill,
    )


def solution(mesh):
    in_specs = (
        P("tm", None),
        P(),
        P(),
        P(None, "mp"),
        P(None, "mp"),
        P(None, "mp"),
        P("mp", None),
        P(None, "mp"),
        P("mp", None),
        P(None, "mp"),
        P(None, "mp"),
        P("tm", None, None),
        P(),
        P(),
    )
    return jax.shard_map(
        on_device, mesh=mesh, in_specs=in_specs, out_specs=P("tm", "mp"), check_vma=False
    )
```

time: 386 us -> 123 us (0.32); the launches traced: 380 us -> 122 us
  waiting for transfers between devices: 163 us -> 0 us
  Pallas kernels: 0 us -> 117 us
  matrix products: 84.5 us -> 0 us
  blocking collectives: 63.2 us -> 0 us
  other arithmetic: 30.4 us -> 0 us
  between operations: 21.1 us -> 0.01 us
  local copies, waits for them, and re-layouts: 12.1 us -> 4.84 us
  starting transfers between devices: 5.18 us -> 0 us
    reduce_scatter x1 -> x0, waiting for transfers between devices: 128 us -> none  [on_device(): lax.psum_scatter(partial_cross.astype(jnp.bfloat16), 'mp', scatter_dimens...]
    pallas_call x0 -> x1, Pallas kernels: none -> 117 us  [on_device(): pl.pallas_call(kernel, out_shape=jax.ShapeDtypeStruct((1024, COLS), BF16)...]
    unnamed x1 -> x0, blocking collectives: 63.2 us -> none
    dot_general x11 -> x0, matrix products: 51 us -> none  [the longest x4 23.1 us: attend(): jnp.einsum('hqk,khd->qhd', probs, value_heads, preferred_element_type=jnp...]
    sub x4 -> x0, matrix products: 33.5 us -> none  [attend(): weights = jnp.exp(scores - top)]
    psum x1 -> x0, waiting for transfers between devices: 19.2 us -> none  [on_device(): lax.psum(partial_self.astype(jnp.bfloat16), 'mp').astype(jnp.float32)]
    all_gather x1 -> x0, waiting for transfers between devices: 16 us -> none  [entering(): gathered = jax.tree.map(lambda a: lax.all_gather(a, axis), part)]
    add x1 -> x0, other arithmetic: 9.15 us -> none  [on_device(): hidden = tokens.astype(jnp.float32) + summed]
  transfers between devices with their start and end apart: 4 -> 0, of which waited for: 3 -> 0; matrix products, arithmetic and copies ran while one was open for 14% -> 0% of each run, Pallas kernels for 0% -> 0%
where the time goes in v1:
time: 123 us; the launch traced here: 122 us
  Pallas kernels  117 us (95%)
  local copies, waits for them, and re-layouts  4.84 us (4%)
    pallas_call x1, Pallas kernels, on_device(): pl.pallas_call(kernel, out_shape=jax.ShapeDtypeStruct((1024, COLS), BF16)...  117 us

profile of v1, /device:TPU:1, one launch (start us, length us, event | category | flops | bytes accessed | tf_op | source)
XLA Modules:
  0.0 122.0 jit_solution(13912454637949490509)
XLA Ops:
  0.0 1.3 %reshape.12.gain_s = bf16[1,2048]{1,0:T(2,128)(2,1)} reshape(bf16[2048]{0:T(1024)(128)(2,1)} %param.15) | data formatting | bytes 8192 | tf_op jit(solution)/shard_map/reshape | solution.py:481
  1.3 1.3 %reshape.13.gain_c = bf16[1,2048]{1,0:T(2,128)(2,1)} reshape(bf16[2048]{0:T(1024)(128)(2,1)} %param.16) | data formatting | bytes 8192 | tf_op jit(solution)/shard_map/reshape | solution.py:481
  2.6 117.2 %shard_map.136 = bf16[1024,512]{1,0:T(8,128)(2,1)} custom-call(bf16[1024,2048]{1,0:T(8,128)(2,1)} %tokens.1, bf16[1,2048]{1,0:T(2,128)(2,1)} %reshape.12.gain_s, bf16[1,2048]{1,0:T(2,128)(2,1)} %reshape.13.gain_c, bf16[2048,512]{1,0:T(8,128)(2,1)} %w_q.1, bf16[2048,512]{1,0:T(8,128)(2,1)} %w_k.1, bf16[2048,512]{1,0:T(8,128)(2,1)} %w_v.1, ...), custom_call_target="tpu_custom_call" | custom-call | tf_op jit(solution)/shard_map/pallas_call | solution.py:471
  119.8 2.3 %copy.16 = bf16[1024,512]{1,0:T(8,128)(2,1)} copy(bf16[1024,512]{1,0:T(8,128)(2,1)} %shard_map.136) | data formatting | bytes 2097152

commit v2 on v1

v2 whole, which is shorter than its diff:
```python
import jax
import jax.numpy as jnp
from jax import lax
from jax.experimental import pallas as pl
from jax.experimental.pallas import tpu as pltpu
from jax.sharding import PartitionSpec as P

F32 = jnp.float32
BF16 = jnp.bfloat16
EPS = 1e-05
MESH = pl.DeviceIdType.MESH
BLK = 512
TILE = 256
COLS = 512
WIDTH = 2048
SUB = TILE // 4
CHUNKS = ((1, 0), (1, 1), (0, 0), (0, 1))
REMOTE = 120


def dot(a, b):
    return jnp.dot(a, b, preferred_element_type=F32)


def dot_t(a, b):
    return lax.dot_general(a, b, (((1,), (1,)), ((), ())), preferred_element_type=F32)


def kernel(
    tokens, gain_s, gain_c, w_q, w_k, w_v, w_o, w_cq, w_co, w_tk, w_tv, text, song, fill,
    out,
    tok, nrm, wq, wk, wv, wo, wcq, wco, wtk, wtv, txt, tin, tsib,
    q, k, v, kp, vp, ctx, hid, own, cs, cr, os_, tk, tv, bias, cc,
    lsem, ssem, rsem,
):
    t, x = lax.axis_index("tm"), lax.axis_index("mp")
    core, y, z = lax.rem(t, 2), t // 8, lax.rem(t // 2, 4)
    right, left, across = lax.rem(x + 1, 4), lax.rem(x + 3, 4), lax.rem(x + 2, 4)
    to_right, to_left, to_across = {"mp": right}, {"mp": left}, {"mp": across}
    up, down = {"tm": lax.rem(t + 8, 32)}, {"tm": lax.rem(t + 24, 32)}
    z_up = {"tm": y * 8 + lax.rem(z + 1, 4) * 2 + core}
    z_down = {"tm": y * 8 + lax.rem(z + 3, 4) * 2 + core}
    next1, prev1 = {"tm": lax.rem(t + 1, 32)}, {"tm": lax.rem(t + 31, 32)}
    sibling = {"tm": t + 1 - 2 * core}

    loads = {}

    def load(name, src, dst):
        copy = pltpu.make_async_copy(src, dst, lsem.at[len(loads)])
        copy.start()
        loads[name] = copy

    def loaded(*names):
        for name in names:
            loads[name].wait()

    barrier = pltpu.get_barrier_semaphore()
    for peer in (prev1, to_right, to_left, to_across, up, down, z_up, z_down, sibling):
        pl.semaphore_signal(barrier, inc=1, device_id=peer, device_id_type=MESH)
    load("tok1", tokens.at[pl.ds(BLK, BLK)], tok.at[pl.ds(BLK, BLK)])
    load("wk", w_k, wk)
    load("wv", w_v, wv)
    load("wq", w_q, wq)
    load("tok0", tokens.at[pl.ds(0, BLK)], tok.at[pl.ds(0, BLK)])
    load("text", text, txt)
    load("wo", w_o, wo.at[x])
    load("wtk", w_tk, wtk)
    load("wtv", w_tv, wtv)
    load("wcq", w_cq, wcq)
    load("wco", w_co, wco.at[x])

    sent = []
    count = [0]

    def fresh():
        count[0] += 1
        return count[0] - 1

    def remote(src, dst, to, n):
        return pltpu.make_async_remote_copy(
            src_ref=src, dst_ref=dst, send_sem=ssem.at[n], recv_sem=rsem.at[n],
            device_id=to, device_id_type=MESH,
        )

    def send(src, dst, to, n):
        copy = remote(src, dst, to, n)
        copy.start()
        sent.append(copy)

    def landed(ref, n):
        remote(ref, ref, to_right, n).wait_recv()

    class Gather:
        def __init__(self, me, after, before, src, at):
            self.me, self.after, self.before, self.src, self.at = me, after, before, src, at
            self.n = [fresh() for _ in range(4)]

        def start(self):
            send(self.src, self.at(self.me, None), self.after, self.n[0])
            send(self.src, self.at(self.me, None), self.before, self.n[1])

        def forward(self):
            lo, hi = lax.rem(self.me + 3, 4), lax.rem(self.me + 1, 4)
            landed(self.at(lo, None), self.n[0])
            send(self.at(lo, 0), self.at(lo, 0), self.after, self.n[2])
            landed(self.at(hi, None), self.n[1])
            send(self.at(hi, 1), self.at(hi, 1), self.before, self.n[3])

        def finish(self):
            far = lax.rem(self.me + 2, 4)
            landed(self.at(far, 0), self.n[2])
            landed(self.at(far, 1), self.n[3])

    def halves(ref, half, size):
        return ref if half is None else ref.at[pl.ds(half * size, size)]

    class Whole:
        def __init__(self, src, full, me, after, before):
            self.full = full
            self.over_x = Gather(
                x, to_right, to_left, src.at[core, me],
                lambda i, h: halves(full.at[i, core, me], h, 32),
            )
            self.groups = (left, right, across)
            self.over_axis = [
                Gather(
                    me, after, before, full.at[g, core, me],
                    lambda i, h, g=g: halves(full.at[g, core, i], h, 32),
                )
                for g in self.groups
            ]
            self.n = [fresh() for _ in range(3)]

        def start(self):
            self.over_x.start()

        def second(self):
            self.over_x.forward()
            self.over_axis[0].start()
            self.over_axis[1].start()

        def third(self):
            self.over_x.finish()
            self.over_axis[2].start()

        def fourth(self, i):
            self.over_axis[i].forward()

        def fifth(self, i):
            self.over_axis[i].finish()
            rows = self.full.at[self.groups[i], core]
            send(rows, rows, sibling, self.n[i])

        def finish(self):
            for i in range(3):
                landed(self.full.at[self.groups[i], 1 - core], self.n[i])

    def strip(i):
        return pl.ds(pl.multiple_of(i * COLS, COLS), COLS)

    whole_o = Whole(w_o, wo, y, up, down)
    whole_co = Whole(w_co, wco, z, z_up, z_down)
    text_n = [fresh() for _ in range(2)]
    kv_n = [fresh() for _ in range(2)]
    ctx_x = [
        Gather(
            x, to_right, to_left, ctx.at[pl.ds(b * BLK + h * TILE, TILE), strip(x)],
            lambda i, part, r=b * BLK + h * TILE: (
                ctx.at[pl.ds(r, TILE), strip(i)]
                if part is None
                else ctx.at[pl.ds(r + part * TILE // 2, TILE // 2), strip(i)]
            ),
        )
        for b, h in CHUNKS
    ]
    cross_n = [[fresh() for _ in range(3)] for _ in CHUNKS]
    out_n = [[fresh() for _ in range(3)] for _ in CHUNKS]

    pl.semaphore_wait(barrier, 9)
    whole_o.start()
    send(text.at[1], tsib, sibling, text_n[0])

    b0 = 2 * t
    s0, s1 = song[b0], song[b0 + 1]
    m1 = song[jnp.maximum(b0 - 1, 0)]
    p2 = song[jnp.minimum(b0 + 2, 63)]
    same = [(t > 0) & (m1 == s0), s0 == s1]
    filled = [
        jnp.where(s0 != s1, fill[s0], BLK),
        jnp.where((t == 31) | (p2 != s1), fill[s1], BLK),
    ]

    def normed(block):
        gain = gain_s[...].astype(F32)

        @pl.loop(0, BLK // 32)
        def _(i):
            values = tok[pl.ds(pl.multiple_of(block * BLK + i * 32, 32), 32), :].astype(F32)
            meansq = jnp.mean(values * values, axis=-1, keepdims=True)
            nrm[pl.ds(pl.multiple_of(i * 32, 32), 32), :] = (
                values * lax.rsqrt(meansq + EPS) * gain
            ).astype(BF16)

    def project(a, w, dst, row, scale=None):
        res = dot(a[...], w[...]).astype(BF16)
        if scale is not None:
            res = res * jnp.asarray(scale, BF16)
        dst[pl.ds(row, a.shape[0]), :] = res

    loaded("tok1")
    normed(1)
    loaded("wk")
    project(nrm, wk, k, BLK)
    send(k.at[pl.ds(BLK, BLK)], kp, next1, kv_n[0])
    loaded("wv")
    project(nrm, wv, v, BLK)
    send(v.at[pl.ds(BLK, BLK)], vp, next1, kv_n[1])
    loaded("wq")
    project(nrm, wq, q, BLK, 0.125)
    whole_o.second()
    whole_co.start()
    loaded("tok0", "text")
    normed(0)
    landed(tsib, text_n[0])

    @pl.when(core == 1)
    def _():
        @pl.loop(0, 4)
        def _(i):
            tsib[i] = jnp.where(same[1], jnp.where(same[0], tsib[i], txt[0, i]), txt[1, i])

        remote(tsib, tin, next1, text_n[1]).start()

    project(nrm, wk, k, 0)
    project(nrm, wv, v, 0)
    whole_o.third()
    project(nrm, wq, q, 0, 0.125)

    lane = lax.broadcasted_iota(jnp.int32, (1, 128), 1)
    pick = [(lane < 64).astype(F32).astype(BF16), (lane >= 64).astype(F32).astype(BF16)]
    ones = jnp.ones((TILE, 128), BF16)

    def softmax_parts(tiles):
        top = tiles[0].max(axis=-1, keepdims=True)
        for s in tiles[1:]:
            top = jnp.maximum(top, s.max(axis=-1, keepdims=True))
        return [jnp.exp(s - top) for s in tiles]

    def with_ones(rows):
        return jnp.concatenate([rows, ones], axis=1)

    def ratio(mixed):
        return mixed[:, :128] / mixed[:, 128:]

    def self_chunk(block, half):
        row = block * BLK + half * TILE
        before_k, before_v = (k, v) if block == 1 else (kp, vp)
        i = lax.broadcasted_iota(jnp.int32, (TILE, BLK), 0) + half * TILE
        j = lax.broadcasted_iota(jnp.int32, (TILE, BLK), 1)
        limit = jnp.where(j <= i, filled[block], jnp.where(same[block], BLK, 0))
        bias[...] = jnp.where(j < limit, 0.0, -1e30)
        lower = lax.broadcasted_iota(jnp.int32, (TILE, TILE), 1) <= lax.broadcasted_iota(
            jnp.int32, (TILE, TILE), 0
        )

        for pair in range(COLS // 128):
            cols = pl.ds(pair * 128, 128)
            queries = q[pl.ds(row, TILE), cols]
            halves_out = []
            for head in range(2):
                query = queries * pick[head]
                scores = []
                for tile in range(2):
                    mine = pl.ds(block * BLK + tile * TILE, TILE)
                    earlier = pl.ds(tile * TILE, TILE)
                    if tile < half:
                        s = dot_t(query, k[mine, cols])
                    elif tile > half:
                        s = dot_t(query, before_k[earlier, cols])
                    else:
                        s = jnp.where(
                            lower,
                            dot_t(query, k[mine, cols]),
                            dot_t(query, before_k[earlier, cols]),
                        )
                    scores.append(s + bias[:, tile * TILE : (tile + 1) * TILE])
                weights = softmax_parts(scores)
                mixed = None
                for tile in range(2):
                    mine = pl.ds(block * BLK + tile * TILE, TILE)
                    earlier = pl.ds(tile * TILE, TILE)
                    w = weights[tile]
                    if tile < half:
                        terms = [(w, v[mine, cols])]
                    elif tile > half:
                        terms = [(w, before_v[earlier, cols])]
                    else:
                        terms = [
                            (jnp.where(lower, w, 0.0), v[mine, cols]),
                            (jnp.where(lower, 0.0, w), before_v[earlier, cols]),
                        ]
                    for a, b in terms:
                        term = dot(a.astype(BF16), with_ones(b))
                        mixed = term if mixed is None else mixed + term
                halves_out.append(ratio(mixed))
            ctx[pl.ds(row, TILE), pl.ds(pl.multiple_of(x * COLS + pair * 128, 128), 128)] = (
                jnp.where(lane < 64, *halves_out).astype(BF16)
            )

    self_chunk(*CHUNKS[0])
    ctx_x[0].start()
    whole_co.second()
    self_chunk(*CHUNKS[1])
    ctx_x[1].start()
    whole_o.fourth(0)
    whole_o.fourth(1)
    landed(kp, kv_n[0])
    landed(vp, kv_n[1])
    self_chunk(*CHUNKS[2])
    ctx_x[0].forward()
    ctx_x[2].start()
    whole_co.third()
    self_chunk(*CHUNKS[3])
    whole_o.fourth(2)
    whole_o.fifth(0)
    whole_o.fifth(1)
    ctx_x[1].forward()
    ctx_x[3].start()

    def choose():
        landed(tin, text_n[1])

        @pl.loop(0, 4)
        def _(i):
            first = jnp.where(same[0], tin[i], txt[0, i])
            txt[0, i] = first
            txt[1, i] = jnp.where(same[1], first, txt[1, i])

    @pl.when(core == 0)
    def _():
        choose()
        remote(txt.at[1], tin, next1, text_n[1]).start()

    whole_o.fifth(2)
    loaded("wo", "wcq")

    def hidden_chunk(c, block, half):
        row = block * BLK + half * TILE
        rows = pl.ds(row, TILE)
        total = jnp.zeros((TILE, 1), F32)
        for i in range(WIDTH // 512):
            cols = pl.ds(i * 512, 512)
            h = tok[rows, cols].astype(F32) + dot(
                ctx[rows, :], wo[:, :, :, :, cols].reshape(WIDTH, 512)
            )
            hid[:, cols] = h
            total = total + jnp.sum(h * h, axis=-1, keepdims=True)
        scale = lax.rsqrt(total * (1.0 / WIDTH) + EPS)
        for i in range(WIDTH // 512):
            cols = pl.ds(i * 512, 512)
            nrm[pl.ds(0, TILE), cols] = (
                hid[:, cols] * scale * gain_c[:, cols].astype(F32)
            ).astype(BF16)
        own[pl.ds(c * SUB, SUB), :] = hid[pl.ds(pl.multiple_of(x * SUB, SUB), SUB), :]
        project(nrm.at[pl.ds(0, TILE)], wcq, cc, 0, 0.125)

    def cross_chunk(c, block, half):
        for pair in range(COLS // 128):
            cols = pl.ds(pair * 128, 128)
            queries = cc[:, cols]
            halves_out = []
            for head in range(2):
                query = queries * pick[head]
                scores = [
                    dot_t(query, tk[block, pl.ds(tile * TILE, TILE), cols]) for tile in range(2)
                ]
                weights = softmax_parts(scores)
                mixed = None
                for tile in range(2):
                    term = dot(
                        weights[tile].astype(BF16),
                        with_ones(tv[block, pl.ds(tile * TILE, TILE), cols]),
                    )
                    mixed = term if mixed is None else mixed + term
                halves_out.append(ratio(mixed))
            cs[c, :, cols] = jnp.where(lane < 64, *halves_out).astype(BF16)
        sub = pl.ds(c * SUB, SUB)
        for to, owner, n in zip(
            (to_across, to_right, to_left), (across, right, left), cross_n[c]
        ):
            rows = pl.ds(pl.multiple_of(owner * SUB, SUB), SUB)
            send(cs.at[c, rows], cr.at[sub, strip(x)], to, n)
        cr[sub, strip(x)] = cs[c, pl.ds(pl.multiple_of(x * SUB, SUB), SUB), :]

    def out_rows(c):
        block, half = CHUNKS[c]
        row = pl.multiple_of(block * BLK + half * TILE + x * SUB, SUB)
        return pl.ds(row, SUB)

    def landing_rows(c, source):
        block, half = CHUNKS[c]
        return pl.ds(pl.multiple_of(block * BLK + half * TILE + source * SUB, SUB), SUB)

    stores = []

    def out_chunks(first, last):
        for c in range(first, last):
            for source, n in zip((across, left, right), cross_n[c]):
                landed(cr.at[pl.ds(c * SUB, SUB), strip(source)], n)
        rows = pl.ds(first * SUB, (last - first) * SUB)
        for d, to in ((2, to_across), (1, to_right), (3, to_left), (0, None)):
            cols = strip(lax.rem(x + d, 4))
            weight = wco[:, :, :, :, cols].reshape(WIDTH, COLS)
            os_[d, rows, :] = (own[rows, cols] + dot(cr[rows, :], weight)).astype(BF16)
            for c in range(first, last):
                piece = os_.at[d, pl.ds(c * SUB, SUB)]
                if to is None:
                    copy = pltpu.make_async_copy(
                        piece, out.at[out_rows(c)], lsem.at[len(loads) + c]
                    )
                    copy.start()
                    stores.append(copy)
                else:
                    send(piece, out.at[out_rows(c)], to, out_n[c][(2, 1, 3).index(d)])

    whole_o.finish()
    ctx_x[0].finish()
    hidden_chunk(0, *CHUNKS[0])
    ctx_x[2].forward()

    @pl.when(core == 1)
    def _():
        choose()

    loaded("wtk", "wtv")
    for block in (1, 0):
        rows = txt[block].reshape(BLK, 1024)
        tk[block] = dot(rows, wtk[...]).astype(BF16)
        tv[block] = dot(rows, wtv[...]).astype(BF16)
    for i in range(3):
        whole_co.fourth(i)
    cross_chunk(0, *CHUNKS[0])
    ctx_x[1].finish()
    hidden_chunk(1, *CHUNKS[1])
    ctx_x[3].forward()
    cross_chunk(1, *CHUNKS[1])
    for i in range(3):
        whole_co.fifth(i)
    ctx_x[2].finish()
    hidden_chunk(2, *CHUNKS[2])
    cross_chunk(2, *CHUNKS[2])
    loaded("wco")
    whole_co.finish()
    out_chunks(0, 2)
    ctx_x[3].finish()
    hidden_chunk(3, *CHUNKS[3])
    cross_chunk(3, *CHUNKS[3])
    out_chunks(2, 3)
    out_chunks(3, 4)
    for c in range(4):
        for source, n in zip((across, left, right), out_n[c]):
            landed(out.at[landing_rows(c, source)], n)
    for copy in sent:
        copy.wait_send()
    remote(tsib, tin, next1, text_n[1]).wait_send()
    for copy in stores:
        copy.wait()


def on_device(
    tokens, gain_self, gain_cross, w_query, w_key, w_value, w_out, w_cross_query, w_cross_out,
    w_text_key, w_text_value, text_states, song_of_block, last_fill,
):
    any_space = pl.BlockSpec(memory_space=pl.ANY)
    vmem = pl.BlockSpec(memory_space=pltpu.VMEM)
    smem = pl.BlockSpec(memory_space=pltpu.SMEM)
    n = len(CHUNKS)

    def buf(*shape, dtype=BF16):
        return pltpu.VMEM(shape, dtype)

    scratch = [
        buf(1024, WIDTH),
        buf(BLK, WIDTH),
        buf(WIDTH, COLS),
        buf(WIDTH, COLS),
        buf(WIDTH, COLS),
        buf(4, 2, 4, 64, WIDTH),
        buf(WIDTH, COLS),
        buf(4, 2, 4, 64, WIDTH),
        buf(1024, COLS),
        buf(1024, COLS),
        buf(2, 4, 128, 1024),
        buf(4, 128, 1024),
        buf(4, 128, 1024),
        buf(1024, COLS),
        buf(1024, COLS),
        buf(1024, COLS),
        buf(BLK, COLS),
        buf(BLK, COLS),
        buf(1024, WIDTH),
        buf(TILE, WIDTH, dtype=F32),
        buf(TILE, WIDTH, dtype=F32),
        buf(n, TILE, COLS),
        buf(TILE, WIDTH),
        buf(4, TILE, COLS),
        buf(2, BLK, COLS),
        buf(2, BLK, COLS),
        buf(TILE, BLK, dtype=F32),
        buf(TILE, COLS),
        pltpu.SemaphoreType.DMA((16,)),
        pltpu.SemaphoreType.DMA((REMOTE,)),
        pltpu.SemaphoreType.DMA((REMOTE,)),
    ]
    return pl.pallas_call(
        kernel,
        out_shape=jax.ShapeDtypeStruct((1024, COLS), BF16),
        in_specs=[any_space, vmem, vmem] + [any_space] * 9 + [smem, smem],
        out_specs=any_space,
        scratch_shapes=scratch,
        compiler_params=pltpu.CompilerParams(
            collective_id=0, has_side_effects=True, vmem_limit_bytes=62 * 2**20
        ),
    )(
        tokens, gain_self.reshape(1, WIDTH), gain_cross.reshape(1, WIDTH), w_query, w_key, w_value,
        w_out.reshape(2, 4, 64, WIDTH), w_cross_query, w_cross_out.reshape(2, 4, 64, WIDTH),
        w_text_key, w_text_value,
        text_states.reshape(2, 4, 128, 1024), song_of_block, last_fill,
    )


def solution(mesh):
    in_specs = (
        P("tm", None),
        P(),
        P(),
        P(None, "mp"),
        P(None, "mp"),
        P(None, "mp"),
        P("mp", None),
        P(None, "mp"),
        P("mp", None),
        P(None, "mp"),
        P(None, "mp"),
        P("tm", None, None),
        P(),
        P(),
    )
    return jax.shard_map(
        on_device, mesh=mesh, in_specs=in_specs, out_specs=P("tm", "mp"), check_vma=False
    )
```

time: 123 us -> 107 us (0.87)
  Pallas kernels: 117 us -> 101 us
    pallas_call x1, Pallas kernels: 117 us -> 101 us  [on_device(): pl.pallas_call(kernel, out_shape=jax.ShapeDtypeStruct((1024, COLS), BF16)...]
where the time goes in v2:
time: 107 us; the launch traced here: 106 us
  Pallas kernels  101 us (94%)
  local copies, waits for them, and re-layouts  4.84 us (5%)
    pallas_call x1, Pallas kernels, on_device(): pl.pallas_call(kernel, out_shape=jax.ShapeDtypeStruct((1024, COLS), BF16)...  101 us
    unnamed x1, local copies, waits for them, and re-layouts  2.26 us

profile of v2, /device:TPU:1, one launch (start us, length us, event | category | flops | bytes accessed | tf_op | source)
XLA Modules:
  0.0 106.2 jit_solution(18420627821432107931)
XLA Ops:
  0.0 1.3 %reshape.15.gain_s = bf16[1,2048]{1,0:T(2,128)(2,1)} reshape(bf16[2048]{0:T(1024)(128)(2,1)} %param.15) | data formatting | bytes 8192 | tf_op jit(solution)/shard_map/reshape | solution.py:525
  1.3 1.3 %reshape.16.gain_c = bf16[1,2048]{1,0:T(2,128)(2,1)} reshape(bf16[2048]{0:T(1024)(128)(2,1)} %param.16) | data formatting | bytes 8192 | tf_op jit(solution)/shard_map/reshape | solution.py:525
  2.6 101.3 %shard_map.136 = bf16[1024,512]{1,0:T(8,128)(2,1)} custom-call(bf16[1024,2048]{1,0:T(8,128)(2,1)} %tokens.1, bf16[1,2048]{1,0:T(2,128)(2,1)} %reshape.15.gain_s, bf16[1,2048]{1,0:T(2,128)(2,1)} %reshape.16.gain_c, bf16[2048,512]{1,0:T(8,128)(2,1)} %w_q.1, bf16[2048,512]{1,0:T(8,128)(2,1)} %w_k.1, bf16[2048,512]{1,0:T(8,128)(2,1)} %w_v.1, ...), custom_call_target="tpu_custom_call" | custom-call | tf_op jit(solution)/shard_map/pallas_call | solution.py:515
  103.9 2.3 %copy.16 = bf16[1024,512]{1,0:T(8,128)(2,1)} copy(bf16[1024,512]{1,0:T(8,128)(2,1)} %shard_map.136) | data formatting | bytes 2097152

commit v3 on v2

--- a/solution.py
+++ b/solution.py
@@ -15,7 +15,8 @@
 WIDTH = 2048
 SUB = TILE // 4
 CHUNKS = ((1, 0), (1, 1), (0, 0), (0, 1))
-REMOTE = 120
+FIRST_O = FIRST_CO = 1024
+REMOTE = 192
 
 
 def dot(a, b):
@@ -37,9 +38,11 @@
     core, y, z = lax.rem(t, 2), t // 8, lax.rem(t // 2, 4)
     right, left, across = lax.rem(x + 1, 4), lax.rem(x + 3, 4), lax.rem(x + 2, 4)
     to_right, to_left, to_across = {"mp": right}, {"mp": left}, {"mp": across}
-    up, down = {"tm": lax.rem(t + 8, 32)}, {"tm": lax.rem(t + 24, 32)}
+    y_up, y_down = {"tm": lax.rem(t + 8, 32)}, {"tm": lax.rem(t + 24, 32)}
+    y_far = {"tm": lax.rem(t + 16, 32)}
     z_up = {"tm": y * 8 + lax.rem(z + 1, 4) * 2 + core}
     z_down = {"tm": y * 8 + lax.rem(z + 3, 4) * 2 + core}
+    z_far = {"tm": y * 8 + lax.rem(z + 2, 4) * 2 + core}
     next1, prev1 = {"tm": lax.rem(t + 1, 32)}, {"tm": lax.rem(t + 31, 32)}
     sibling = {"tm": t + 1 - 2 * core}
 
@@ -55,19 +58,11 @@
             loads[name].wait()
 
     barrier = pltpu.get_barrier_semaphore()
-    for peer in (prev1, to_right, to_left, to_across, up, down, z_up, z_down, sibling):
+    peers = (prev1, to_right, to_left, to_across, y_up, y_down, y_far, z_up, z_down, z_far, sibling)
+    for peer in peers:
         pl.semaphore_signal(barrier, inc=1, device_id=peer, device_id_type=MESH)
     load("tok1", tokens.at[pl.ds(BLK, BLK)], tok.at[pl.ds(BLK, BLK)])
     load("wk", w_k, wk)
-    load("wv", w_v, wv)
-    load("wq", w_q, wq)
-    load("tok0", tokens.at[pl.ds(0, BLK)], tok.at[pl.ds(0, BLK)])
-    load("text", text, txt)
-    load("wo", w_o, wo.at[x])
-    load("wtk", w_tk, wtk)
-    load("wtv", w_tv, wtv)
-    load("wcq", w_cq, wcq)
-    load("wco", w_co, wco.at[x])
 
     sent = []
     count = [0]
@@ -91,94 +86,119 @@
         remote(ref, ref, to_right, n).wait_recv()
 
     class Gather:
-        def __init__(self, me, after, before, src, at):
-            self.me, self.after, self.before, self.src, self.at = me, after, before, src, at
+        def __init__(self, row):
+            self.row = row
             self.n = [fresh() for _ in range(4)]
 
+        def at(self, d, half=None):
+            if half is None:
+                return ctx.at[pl.ds(self.row, TILE), pl.ds(d * COLS, COLS)]
+            rows = pl.ds(self.row + half * TILE // 2, TILE // 2)
+            return ctx.at[rows, pl.ds(d * COLS, COLS)]
+
         def start(self):
-            send(self.src, self.at(self.me, None), self.after, self.n[0])
-            send(self.src, self.at(self.me, None), self.before, self.n[1])
+            send(self.at(0), self.at(3), to_right, self.n[0])
+            send(self.at(0), self.at(1), to_left, self.n[1])
 
         def forward(self):
-            lo, hi = lax.rem(self.me + 3, 4), lax.rem(self.me + 1, 4)
-            landed(self.at(lo, None), self.n[0])
-            send(self.at(lo, 0), self.at(lo, 0), self.after, self.n[2])
-            landed(self.at(hi, None), self.n[1])
-            send(self.at(hi, 1), self.at(hi, 1), self.before, self.n[3])
+            landed(self.at(3), self.n[0])
+            send(self.at(3, 0), self.at(2, 0), to_right, self.n[2])
+            landed(self.at(1), self.n[1])
+            send(self.at(1, 1), self.at(2, 1), to_left, self.n[3])
 
         def finish(self):
-            far = lax.rem(self.me + 2, 4)
-            landed(self.at(far, 0), self.n[2])
-            landed(self.at(far, 1), self.n[3])
-
-    def halves(ref, half, size):
-        return ref if half is None else ref.at[pl.ds(half * size, size)]
+            landed(self.at(2, 0), self.n[2])
+            landed(self.at(2, 1), self.n[3])
 
     class Whole:
-        def __init__(self, src, full, me, after, before):
-            self.full = full
-            self.over_x = Gather(
-                x, to_right, to_left, src.at[core, me],
-                lambda i, h: halves(full.at[i, core, me], h, 32),
+        def __init__(self, src, full, first):
+            self.src, self.full = src, full
+            self.n = iter([fresh() for _ in range(64)])
+            self.parts = (
+                (pl.ds(0, first), y, (y_up, y_down, y_far), z, (z_up, z_down)),
+                (pl.ds(first, WIDTH - first), z, (z_up, z_down, z_far), y, (y_up, y_down)),
             )
-            self.groups = (left, right, across)
-            self.over_axis = [
-                Gather(
-                    me, after, before, full.at[g, core, me],
-                    lambda i, h, g=g: halves(full.at[g, core, i], h, 32),
-                )
-                for g in self.groups
-            ]
-            self.n = [fresh() for _ in range(3)]
+            self.waits, self.late, self.last = [], ([], []), []
+
+        def ref(self, part, axis, at_first, at_second):
+            cols = self.parts[part][0]
+            at_y, at_z = (at_first, at_second) if part == 0 else (at_second, at_first)
+            return self.full.at[pl.ds(1, 3), core, at_y, at_z, :, cols]
+
+        def send(self, src, dst, to):
+            n = next(self.n)
+            send(src, dst, to, n)
+            return n
+
+        def arrived(self):
+            for ref, n in self.waits:
+                landed(ref, n)
+            self.waits = []
 
         def start(self):
-            self.over_x.start()
+            piece = self.src.at[core, y, z]
+            for d, to in ((3, to_right), (1, to_left), (2, to_across)):
+                spot = self.full.at[d, core, y, z]
+                self.waits.append((spot, self.send(piece, spot, to)))
 
         def second(self):
-            self.over_x.forward()
-            self.over_axis[0].start()
-            self.over_axis[1].start()
+            self.arrived()
+            for i, (_, one, (up, down, far), two, _) in enumerate(self.parts):
+                spot = self.ref(i, 0, one, two)
+                for to, back in ((up, 3), (down, 1), (far, 2)):
+                    n = self.send(spot, spot, to)
+                    self.waits.append((self.ref(i, 0, lax.rem(one + back, 4), two), n))
 
         def third(self):
-            self.over_x.finish()
-            self.over_axis[2].start()
+            self.arrived()
+            for i, (_, _, _, two, (up, down)) in enumerate(self.parts):
+                spot = self.ref(i, 1, pl.ds(0, 4), two)
+                for to, back in ((up, 3), (down, 1)):
+                    n = self.send(spot, spot, to)
+                    self.waits.append((self.ref(i, 1, pl.ds(0, 4), lax.rem(two + back, 4)), n))
 
         def fourth(self, i):
-            self.over_axis[i].forward()
+            _, _, _, two, (up, down) = self.parts[i]
+            for ref, n in self.waits[2 * i : 2 * i + 2]:
+                landed(ref, n)
+            far = lax.rem(two + 2, 4)
+            for to, back, half in ((up, 3, pl.ds(0, 2)), (down, 1, pl.ds(2, 2))):
+                spot = self.ref(i, 1, half, lax.rem(two + back, 4))
+                n = self.send(spot, spot, to)
+                self.late[i].append((self.ref(i, 1, half, far), n))
+            for back in (0, 1, 3):
+                self.share(i, lax.rem(two + back, 4))
+
+        def share(self, i, at):
+            at_y, at_z = (pl.ds(0, 4), at) if i == 0 else (at, pl.ds(0, 4))
+            cols = self.parts[i][0]
+            spot = self.full.at[pl.ds(1, 3), core, at_y, at_z, :, cols]
+            n = self.send(spot, spot, sibling)
+            self.last.append((self.full.at[pl.ds(1, 3), 1 - core, at_y, at_z, :, cols], n))
 
         def fifth(self, i):
-            self.over_axis[i].finish()
-            rows = self.full.at[self.groups[i], core]
-            send(rows, rows, sibling, self.n[i])
+            for ref, n in self.late[i]:
+                landed(ref, n)
+            self.share(i, lax.rem(self.parts[i][3] + 2, 4))
 
         def finish(self):
-            for i in range(3):
-                landed(self.full.at[self.groups[i], 1 - core], self.n[i])
+            for ref, n in self.last:
+                landed(ref, n)
 
     def strip(i):
         return pl.ds(pl.multiple_of(i * COLS, COLS), COLS)
 
-    whole_o = Whole(w_o, wo, y, up, down)
-    whole_co = Whole(w_co, wco, z, z_up, z_down)
-    text_n = [fresh() for _ in range(2)]
+    whole_o = Whole(w_o, wo, FIRST_O)
+    whole_co = Whole(w_co, wco, FIRST_CO)
+    text_n = [fresh() for _ in range(6)]
     kv_n = [fresh() for _ in range(2)]
     ctx_x = [
-        Gather(
-            x, to_right, to_left, ctx.at[pl.ds(b * BLK + h * TILE, TILE), strip(x)],
-            lambda i, part, r=b * BLK + h * TILE: (
-                ctx.at[pl.ds(r, TILE), strip(i)]
-                if part is None
-                else ctx.at[pl.ds(r + part * TILE // 2, TILE // 2), strip(i)]
-            ),
-        )
+        Gather(b * BLK + h * TILE)
         for b, h in CHUNKS
     ]
     cross_n = [[fresh() for _ in range(3)] for _ in CHUNKS]
     out_n = [[fresh() for _ in range(3)] for _ in CHUNKS]
 
-    pl.semaphore_wait(barrier, 9)
-    whole_o.start()
-    send(text.at[1], tsib, sibling, text_n[0])
 
     b0 = 2 * t
     s0, s1 = song[b0], song[b0 + 1]
@@ -191,7 +211,7 @@
     ]
 
     def normed(block):
-        gain = gain_s[...].astype(F32)
+        gain = gain_s[...].astype(F32).reshape(1, WIDTH)
 
         @pl.loop(0, BLK // 32)
         def _(i):
@@ -208,32 +228,33 @@
         dst[pl.ds(row, a.shape[0]), :] = res
 
     loaded("tok1")
+    load("wv", w_v, wv)
     normed(1)
     loaded("wk")
+    load("wq", w_q, wq)
+    load("tok0", tokens.at[pl.ds(0, BLK)], tok.at[pl.ds(0, BLK)])
     project(nrm, wk, k, BLK)
+    loaded("wv")
+    load("text", text, txt)
+    project(nrm, wv, v, BLK)
+    pl.semaphore_wait(barrier, 11)
+    whole_o.start()
     send(k.at[pl.ds(BLK, BLK)], kp, next1, kv_n[0])
-    loaded("wv")
-    project(nrm, wv, v, BLK)
     send(v.at[pl.ds(BLK, BLK)], vp, next1, kv_n[1])
+    send(text.at[1], tsib, sibling, text_n[0])
     loaded("wq")
     project(nrm, wq, q, BLK, 0.125)
+    loaded("tok0", "text")
+    load("wo", w_o, wo.at[0])
+    load("wtk", w_tk, wtk)
+    load("wtv", w_tv, wtv)
+    load("wcq", w_cq, wcq)
+    load("wco", w_co, wco.at[0])
+    normed(0)
+    project(nrm, wk, k, 0)
     whole_o.second()
     whole_co.start()
-    loaded("tok0", "text")
-    normed(0)
-    landed(tsib, text_n[0])
-
-    @pl.when(core == 1)
-    def _():
-        @pl.loop(0, 4)
-        def _(i):
-            tsib[i] = jnp.where(same[1], jnp.where(same[0], tsib[i], txt[0, i]), txt[1, i])
-
-        remote(tsib, tin, next1, text_n[1]).start()
-
-    project(nrm, wk, k, 0)
     project(nrm, wv, v, 0)
-    whole_o.third()
     project(nrm, wq, q, 0, 0.125)
 
     lane = lax.broadcasted_iota(jnp.int32, (1, 128), 1)
@@ -303,33 +324,44 @@
                         term = dot(a.astype(BF16), with_ones(b))
                         mixed = term if mixed is None else mixed + term
                 halves_out.append(ratio(mixed))
-            ctx[pl.ds(row, TILE), pl.ds(pl.multiple_of(x * COLS + pair * 128, 128), 128)] = (
-                jnp.where(lane < 64, *halves_out).astype(BF16)
-            )
+            ctx[pl.ds(row, TILE), cols] = jnp.where(lane < 64, *halves_out).astype(BF16)
 
     self_chunk(*CHUNKS[0])
     ctx_x[0].start()
-    whole_co.second()
+    landed(tsib, text_n[0])
+
+    @pl.when(core == 1)
+    def _():
+        piece = jnp.where(same[0], tsib[x], txt[0, x])
+        tsib[x] = jnp.where(same[1], piece, txt[1, x])
+        remote(tsib.at[x], tin.at[x], next1, text_n[1]).start()
+
     self_chunk(*CHUNKS[1])
     ctx_x[1].start()
-    whole_o.fourth(0)
-    whole_o.fourth(1)
+    whole_o.third()
     landed(kp, kv_n[0])
     landed(vp, kv_n[1])
     self_chunk(*CHUNKS[2])
+    ctx_x[2].start()
+
+    @pl.when(core == 0)
+    def _():
+        landed(tin.at[x], text_n[1])
+        for to, n in zip((to_across, to_right, to_left), text_n[2:]):
+            remote(tin.at[x], tin.at[x], to, n).start()
+
+    self_chunk(*CHUNKS[3])
+    ctx_x[3].start()
     ctx_x[0].forward()
-    ctx_x[2].start()
-    whole_co.third()
-    self_chunk(*CHUNKS[3])
-    whole_o.fourth(2)
+    whole_o.fourth(1)
+    whole_o.fourth(0)
+    whole_co.second()
+    ctx_x[1].forward()
+    whole_o.fifth(1)
     whole_o.fifth(0)
-    whole_o.fifth(1)
-    ctx_x[1].forward()
-    ctx_x[3].start()
+    ctx_x[2].forward()
 
     def choose():
-        landed(tin, text_n[1])
-
         @pl.loop(0, 4)
         def _(i):
             first = jnp.where(same[0], tin[i], txt[0, i])
@@ -338,11 +370,10 @@
 
     @pl.when(core == 0)
     def _():
+        for source, n in zip((across, left, right), text_n[2:]):
+            landed(tin.at[source], n)
         choose()
-        remote(txt.at[1], tin, next1, text_n[1]).start()
-
-    whole_o.fifth(2)
-    loaded("wo", "wcq")
+        remote(txt.at[1], tin, sibling, text_n[5]).start()
 
     def hidden_chunk(c, block, half):
         row = block * BLK + half * TILE
@@ -351,7 +382,7 @@
         for i in range(WIDTH // 512):
             cols = pl.ds(i * 512, 512)
             h = tok[rows, cols].astype(F32) + dot(
-                ctx[rows, :], wo[:, :, :, :, cols].reshape(WIDTH, 512)
+                ctx[rows, :], wo[:, :, :, :, :, cols].reshape(WIDTH, 512)
             )
             hid[:, cols] = h
             total = total + jnp.sum(h * h, axis=-1, keepdims=True)
@@ -359,7 +390,7 @@
         for i in range(WIDTH // 512):
             cols = pl.ds(i * 512, 512)
             nrm[pl.ds(0, TILE), cols] = (
-                hid[:, cols] * scale * gain_c[:, cols].astype(F32)
+                hid[:, cols] * scale * gain_c[cols].astype(F32).reshape(1, 512)
             ).astype(BF16)
         own[pl.ds(c * SUB, SUB), :] = hid[pl.ds(pl.multiple_of(x * SUB, SUB), SUB), :]
         project(nrm.at[pl.ds(0, TILE)], wcq, cc, 0, 0.125)
@@ -385,12 +416,10 @@
                 halves_out.append(ratio(mixed))
             cs[c, :, cols] = jnp.where(lane < 64, *halves_out).astype(BF16)
         sub = pl.ds(c * SUB, SUB)
-        for to, owner, n in zip(
-            (to_across, to_right, to_left), (across, right, left), cross_n[c]
-        ):
-            rows = pl.ds(pl.multiple_of(owner * SUB, SUB), SUB)
-            send(cs.at[c, rows], cr.at[sub, strip(x)], to, n)
-        cr[sub, strip(x)] = cs[c, pl.ds(pl.multiple_of(x * SUB, SUB), SUB), :]
+        for d, to, n in zip((2, 1, 3), (to_across, to_right, to_left), cross_n[c]):
+            rows = pl.ds(pl.multiple_of(lax.rem(x + d, 4) * SUB, SUB), SUB)
+            send(cs.at[c, rows], cr.at[sub, pl.ds((4 - d) * COLS, COLS)], to, n)
+        cr[sub, pl.ds(0, COLS)] = cs[c, pl.ds(pl.multiple_of(x * SUB, SUB), SUB), :]
 
     def out_rows(c):
         block, half = CHUNKS[c]
@@ -405,12 +434,12 @@
 
     def out_chunks(first, last):
         for c in range(first, last):
-            for source, n in zip((across, left, right), cross_n[c]):
-                landed(cr.at[pl.ds(c * SUB, SUB), strip(source)], n)
+            for d, n in zip((2, 3, 1), cross_n[c]):
+                landed(cr.at[pl.ds(c * SUB, SUB), pl.ds(d * COLS, COLS)], n)
         rows = pl.ds(first * SUB, (last - first) * SUB)
         for d, to in ((2, to_across), (1, to_right), (3, to_left), (0, None)):
             cols = strip(lax.rem(x + d, 4))
-            weight = wco[:, :, :, :, cols].reshape(WIDTH, COLS)
+            weight = wco[:, :, :, :, :, cols].reshape(WIDTH, COLS)
             os_[d, rows, :] = (own[rows, cols] + dot(cr[rows, :], weight)).astype(BF16)
             for c in range(first, last):
                 piece = os_.at[d, pl.ds(c * SUB, SUB)]
@@ -423,13 +452,12 @@
                 else:
                     send(piece, out.at[out_rows(c)], to, out_n[c][(2, 1, 3).index(d)])
 
-    whole_o.finish()
-    ctx_x[0].finish()
-    hidden_chunk(0, *CHUNKS[0])
-    ctx_x[2].forward()
+    whole_co.third()
+    ctx_x[3].forward()
 
     @pl.when(core == 1)
     def _():
+        landed(tin, text_n[5])
         choose()
 
     loaded("wtk", "wtv")
@@ -437,15 +465,18 @@
         rows = txt[block].reshape(BLK, 1024)
         tk[block] = dot(rows, wtk[...]).astype(BF16)
         tv[block] = dot(rows, wtv[...]).astype(BF16)
-    for i in range(3):
-        whole_co.fourth(i)
+    loaded("wo", "wcq")
+    whole_o.finish()
+    ctx_x[0].finish()
+    hidden_chunk(0, *CHUNKS[0])
     cross_chunk(0, *CHUNKS[0])
+    whole_co.fourth(1)
+    whole_co.fourth(0)
     ctx_x[1].finish()
     hidden_chunk(1, *CHUNKS[1])
-    ctx_x[3].forward()
     cross_chunk(1, *CHUNKS[1])
-    for i in range(3):
-        whole_co.fifth(i)
+    whole_co.fifth(1)
+    whole_co.fifth(0)
     ctx_x[2].finish()
     hidden_chunk(2, *CHUNKS[2])
     cross_chunk(2, *CHUNKS[2])
@@ -462,7 +493,17 @@
             landed(out.at[landing_rows(c, source)], n)
     for copy in sent:
         copy.wait_send()
-    remote(tsib, tin, next1, text_n[1]).wait_send()
+
+    @pl.when(core == 1)
+    def _():
+        remote(tsib.at[x], tin.at[x], next1, text_n[1]).wait_send()
+
+    @pl.when(core == 0)
+    def _():
+        for to, n in zip((to_across, to_right, to_left), text_n[2:]):
+            remote(tin.at[x], tin.at[x], to, n).wait_send()
+        remote(txt.at[1], tin, sibling, text_n[5]).wait_send()
+
     for copy in stores:
         copy.wait()
 
@@ -485,9 +526,9 @@
         buf(WIDTH, COLS),
         buf(WIDTH, COLS),
         buf(WIDTH, COLS),
-        buf(4, 2, 4, 64, WIDTH),
+        buf(4, 2, 4, 4, 16, WIDTH),
         buf(WIDTH, COLS),
-        buf(4, 2, 4, 64, WIDTH),
+        buf(4, 2, 4, 4, 16, WIDTH),
         buf(1024, COLS),
         buf(1024, COLS),
         buf(2, 4, 128, 1024),
@@ -522,8 +563,8 @@
             collective_id=0, has_side_effects=True, vmem_limit_bytes=62 * 2**20
         ),
     )(
-        tokens, gain_self.reshape(1, WIDTH), gain_cross.reshape(1, WIDTH), w_query, w_key, w_value,
-        w_out.reshape(2, 4, 64, WIDTH), w_cross_query, w_cross_out.reshape(2, 4, 64, WIDTH),
+        tokens, gain_self, gain_cross, w_query, w_key, w_value,
+        w_out.reshape(2, 4, 4, 16, WIDTH), w_cross_query, w_cross_out.reshape(2, 4, 4, 16, WIDTH),
         w_text_key, w_text_value,
         text_states.reshape(2, 4, 128, 1024), song_of_block, last_fill,
     )

time: 107 us -> 98.9 us (0.924)
  Pallas kernels: 101 us -> 95 us
  local copies, waits for them, and re-layouts: 4.84 us -> 2.26 us
    pallas_call x1, Pallas kernels: 101 us -> 95 us  [on_device(): pl.pallas_call(kernel, out_shape=jax.ShapeDtypeStruct((1024, COLS), BF16)...]
    reshape x2 -> x0, local copies, waits for them, and re-layouts: 2.57 us -> none  [the longest x1 1.29 us: on_device(): gain_self.reshape(1, WIDTH)]
where the time goes in v3:
time: 98.9 us; the launch traced here: 97.3 us
  Pallas kernels  95 us (96%)
  local copies, waits for them, and re-layouts  2.26 us (2%)
    pallas_call x1, Pallas kernels, on_device(): pl.pallas_call(kernel, out_shape=jax.ShapeDtypeStruct((1024, COLS), BF16)...  95 us
    unnamed x1, local copies, waits for them, and re-layouts  2.26 us

profile of v3, /device:TPU:1, one launch (start us, length us, event | category | flops | bytes accessed | tf_op | source)
XLA Modules:
  0.0 97.3 jit_solution(13887667812105412006)
XLA Ops:
  0.0 95.0 %shard_map.136 = bf16[1024,512]{1,0:T(8,128)(2,1)} custom-call(bf16[1024,2048]{1,0:T(8,128)(2,1)} %tokens.1, bf16[2048]{0:T(1024)(128)(2,1)} %gain_s.1, bf16[2048]{0:T(1024)(128)(2,1)} %gain_c.1, bf16[2048,512]{1,0:T(8,128)(2,1)} %w_q.1, bf16[2048,512]{1,0:T(8,128)(2,1)} %w_k.1, bf16[2048,512]{1,0:T(8,128)(2,1)} %w_v.1, ...), custom_call_target="tpu_custom_call" | custom-call | tf_op jit(solution)/shard_map/pallas_call | solution.py:556
  95.0 2.3 %copy.16 = bf16[1024,512]{1,0:T(8,128)(2,1)} copy(bf16[1024,512]{1,0:T(8,128)(2,1)} %shard_map.136) | data formatting | bytes 2097152

commit v4 on v3

--- a/solution.py
+++ b/solution.py
@@ -15,7 +15,7 @@
 WIDTH = 2048
 SUB = TILE // 4
 CHUNKS = ((1, 0), (1, 1), (0, 0), (0, 1))
-FIRST_O = FIRST_CO = 1024
+FIRST_O, FIRST_CO = 1280, 1024
 REMOTE = 192
 
 
@@ -236,10 +236,10 @@
     project(nrm, wk, k, BLK)
     loaded("wv")
     load("text", text, txt)
-    project(nrm, wv, v, BLK)
     pl.semaphore_wait(barrier, 11)
     whole_o.start()
     send(k.at[pl.ds(BLK, BLK)], kp, next1, kv_n[0])
+    project(nrm, wv, v, BLK)
     send(v.at[pl.ds(BLK, BLK)], vp, next1, kv_n[1])
     send(text.at[1], tsib, sibling, text_n[0])
     loaded("wq")
@@ -452,9 +452,6 @@
                 else:
                     send(piece, out.at[out_rows(c)], to, out_n[c][(2, 1, 3).index(d)])
 
-    whole_co.third()
-    ctx_x[3].forward()
-
     @pl.when(core == 1)
     def _():
         landed(tin, text_n[5])
@@ -465,26 +462,28 @@
         rows = txt[block].reshape(BLK, 1024)
         tk[block] = dot(rows, wtk[...]).astype(BF16)
         tv[block] = dot(rows, wtv[...]).astype(BF16)
+    whole_co.third()
     loaded("wo", "wcq")
     whole_o.finish()
     ctx_x[0].finish()
     hidden_chunk(0, *CHUNKS[0])
+    ctx_x[3].forward()
     cross_chunk(0, *CHUNKS[0])
-    whole_co.fourth(1)
-    whole_co.fourth(0)
     ctx_x[1].finish()
     hidden_chunk(1, *CHUNKS[1])
     cross_chunk(1, *CHUNKS[1])
-    whole_co.fifth(1)
-    whole_co.fifth(0)
+    whole_co.fourth(1)
+    whole_co.fourth(0)
     ctx_x[2].finish()
     hidden_chunk(2, *CHUNKS[2])
     cross_chunk(2, *CHUNKS[2])
+    whole_co.fifth(1)
+    whole_co.fifth(0)
+    ctx_x[3].finish()
+    hidden_chunk(3, *CHUNKS[3])
     loaded("wco")
     whole_co.finish()
     out_chunks(0, 2)
-    ctx_x[3].finish()
-    hidden_chunk(3, *CHUNKS[3])
     cross_chunk(3, *CHUNKS[3])
     out_chunks(2, 3)
     out_chunks(3, 4)

time: 98.9 us -> 99.9 us (1.010); the launches traced: 97.3 us -> 99.7 us
  Pallas kernels: 95 us -> 97.5 us
    pallas_call x1, Pallas kernels: 95 us -> 97.5 us  [on_device(): pl.pallas_call(kernel, out_shape=jax.ShapeDtypeStruct((1024, COLS), BF16)...]
where the time goes in v4:
time: 99.9 us; the launch traced here: 99.7 us
  Pallas kernels  97.5 us (98%)
  local copies, waits for them, and re-layouts  2.26 us (2%)
    pallas_call x1, Pallas kernels, on_device(): pl.pallas_call(kernel, out_shape=jax.ShapeDtypeStruct((1024, COLS), BF16)...  97.5 us
    unnamed x1, local copies, waits for them, and re-layouts  2.26 us

profile of v4, /device:TPU:1, one launch (start us, length us, event | category | flops | bytes accessed | tf_op | source)
XLA Modules:
  0.0 99.7 jit_solution(8426053142234352709)
XLA Ops:
  0.0 97.5 %shard_map.136 = bf16[1024,512]{1,0:T(8,128)(2,1)} custom-call(bf16[1024,2048]{1,0:T(8,128)(2,1)} %tokens.1, bf16[2048]{0:T(1024)(128)(2,1)} %gain_s.1, bf16[2048]{0:T(1024)(128)(2,1)} %gain_c.1, bf16[2048,512]{1,0:T(8,128)(2,1)} %w_q.1, bf16[2048,512]{1,0:T(8,128)(2,1)} %w_k.1, bf16[2048,512]{1,0:T(8,128)(2,1)} %w_v.1, ...), custom_call_target="tpu_custom_call" | custom-call | tf_op jit(solution)/shard_map/pallas_call | solution.py:555
  97.5 2.3 %copy.16 = bf16[1024,512]{1,0:T(8,128)(2,1)} copy(bf16[1024,512]{1,0:T(8,128)(2,1)} %shard_map.136) | data formatting | bytes 2097152
